TPU v7x, 256 devices: a whole 4x4x8 slice. The times are simulated.
256 devices in a mesh: replica: 4 (over x), section: 16 (over z_hi, y, core), tensor: 4 (over z_lo).
Axes of the slice: x: 4, y: 4, z: 8 (z_hi: 2, z_lo: 4; z = z_hi * 4 + z_lo), core: 2. Of those that a mesh axis runs over, the one named last changes fastest.
Arguments:
- enc_hidden: bfloat16 [4, 512, 4096], P('replica', ('section', 'tensor')), may hold values from -6 to 6
- enc_gain: bfloat16 [4, 4096], P('replica'), may hold values from 0.5 to 1.5
- key_weight: bfloat16 [4, 16, 4096, 2048], P('replica', 'section', None, 'tensor'), may hold values from -0.09375 to 0.09375
- value_weight: bfloat16 [4, 16, 4096, 2048], P('replica', 'section', None, 'tensor'), may hold values from -0.09375 to 0.09375
- queries: bfloat16 [4, 16, 256, 2048], P('replica', 'section', None, 'tensor'), may hold values from -360 to 360
- cotangent: bfloat16 [4, 16, 256, 2048], P('replica', 'section', None, 'tensor'), may hold values from -24 to 24
- enc_len: int32 [4], P('replica'), may hold values from 128 to 512, as said below
- dec_len: int32 [4], P('replica'), may hold values from 64 to 256, as said below
Outputs:
- d_queries: bfloat16 [4, 16, 256, 2048], P('replica', 'section', None, 'tensor')
- d_key_weight: bfloat16 [16, 4096, 2048], P('section', 'replica', 'tensor')
- d_value_weight: bfloat16 [16, 4096, 2048], P('section', 'replica', 'tensor')
- hidden_state_gradient: bfloat16 [4, 512, 4096], P('replica', ('section', 'tensor'))
- d_gain: float32 [4096], replicated
Inputs may be any that keep to these rules, and one draw needn't show every extreme that they name: `enc_len`: one replica has all 512 positions, another 512 // 4. `dec_len`: one replica has all 256 tokens, another 256 // 4.
All inputs are finite; a program needn't handle non-finite values.
Results may differ from a plain program's by a relative error of at most 0.017.
The roundings to bfloat16 on the way count: a program that leaves them out, or rounds other values in their place, can miss the bound.
Values may be sent and summed in bfloat16 or wider, within the bound.
A program may use at most 128 MiB of HBM per device.

v0:
```python
import jax
import jax.numpy as jnp
from jax import lax
from jax.sharding import PartitionSpec as P

HD = 256


def attend_back(query_rows, grad_rows, key_rows, value_rows, enc_count, dec_count):
    scale = HD ** (-0.5)
    dec_rows = query_rows.shape[0]
    enc_rows = key_rows.shape[0]
    width = query_rows.shape[1]
    local_heads = width // HD
    query_heads = query_rows.reshape(dec_rows, local_heads, HD)
    key_heads = key_rows.reshape(enc_rows, local_heads, HD)
    value_heads = value_rows.reshape(enc_rows, local_heads, HD)
    keep = (jnp.arange(enc_rows) < enc_count)[None, None, :]
    scores = (
        jnp.einsum("qhd,khd->hqk", query_heads, key_heads, preferred_element_type=jnp.float32)
        * scale
    )
    scores = jnp.where(keep, scores, -1e30)
    top = jnp.max(scores, axis=-1, keepdims=True)
    expo = jnp.where(keep, jnp.exp(scores - top), 0.0)
    probs = expo / jnp.sum(expo, axis=-1, keepdims=True)
    live = (jnp.arange(dec_rows) < dec_count)[:, None]
    grad_in = jnp.where(live, grad_rows, jnp.zeros_like(grad_rows))
    grad_heads = grad_in.reshape(dec_rows, local_heads, HD)
    dprob = jnp.einsum("qhd,khd->hqk", grad_heads, value_heads, preferred_element_type=jnp.float32)
    dscore = probs * (dprob - jnp.sum(probs * dprob, axis=-1, keepdims=True))
    dscore_b = dscore.astype(jnp.bfloat16)
    probs_b = probs.astype(jnp.bfloat16)
    d_query = (
        jnp.einsum("hqk,khd->qhd", dscore_b, key_heads, preferred_element_type=jnp.float32) * scale
    )
    d_key = (
        jnp.einsum("hqk,qhd->khd", dscore_b, query_heads, preferred_element_type=jnp.float32)
        * scale
    )
    d_value = jnp.einsum("hqk,qhd->khd", probs_b, grad_heads, preferred_element_type=jnp.float32)
    d_query = d_query.reshape(dec_rows, width).astype(jnp.bfloat16)
    d_key = d_key.reshape(enc_rows, width).astype(jnp.bfloat16)
    d_value = d_value.reshape(enc_rows, width).astype(jnp.bfloat16)
    return (d_query, d_key, d_value)


def local(enc_hidden, enc_gain, key_weight, value_weight, queries, cotangent, enc_len, dec_len):
    encoder_hidden_state = enc_hidden[0].astype(jnp.float32)
    root_mean_square = jnp.sqrt(
        jnp.mean(encoder_hidden_state * encoder_hidden_state, axis=-1, keepdims=True) + 1e-06
    )
    unit_normalized_input = encoder_hidden_state / root_mean_square
    norm_gain_vector = enc_gain[0].astype(jnp.float32)
    normalized_hidden = (unit_normalized_input * norm_gain_vector).astype(jnp.bfloat16)
    whole = lax.all_gather(normalized_hidden, ("section", "tensor"), axis=0, tiled=True)
    w_key = key_weight[0, 0]
    w_value = value_weight[0, 0]
    key_rows = jnp.dot(whole, w_key, preferred_element_type=jnp.float32).astype(jnp.bfloat16)
    value_rows = jnp.dot(whole, w_value, preferred_element_type=jnp.float32).astype(jnp.bfloat16)
    d_query, d_key, d_value = attend_back(
        queries[0, 0], cotangent[0, 0], key_rows, value_rows, enc_len[0], dec_len[0]
    )
    width = w_key.shape[1]
    replicas = lax.axis_size("replica")
    both_grads = jnp.concatenate([d_key, d_value], axis=1)
    contract_rows = (((0,), (0,)), ((), ()))
    full_grads = lax.dot_general(
        whole, both_grads, contract_rows, preferred_element_type=jnp.float32
    )
    summed = lax.psum_scatter(
        full_grads.astype(jnp.bfloat16), "replica", scatter_dimension=0, tiled=True
    ).astype(jnp.float32)
    d_key_weight = (summed[:, :width] / replicas).astype(jnp.bfloat16)[None]
    d_value_weight = (summed[:, width:] / replicas).astype(jnp.bfloat16)[None]
    contract_cols = (((1,), (1,)), ((), ()))
    term = lax.dot_general(d_key, w_key, contract_cols, preferred_element_type=jnp.float32)
    normalized_gradient = lax.psum_scatter(
        term + lax.dot_general(d_value, w_value, contract_cols, preferred_element_type=jnp.float32),
        ("section", "tensor"),
        scatter_dimension=0,
        tiled=True,
    )
    gain_gradient_terms = jnp.sum(normalized_gradient * unit_normalized_input, axis=0)
    d_gain = lax.psum(gain_gradient_terms, ("replica", "section", "tensor")) / replicas
    scaled_gradient = norm_gain_vector * normalized_gradient
    hidden_state_gradient = (
        scaled_gradient
        - unit_normalized_input
        * jnp.mean(scaled_gradient * unit_normalized_input, axis=-1, keepdims=True)
    ) / root_mean_square
    return (
        d_query[None, None],
        d_key_weight,
        d_value_weight,
        hidden_state_gradient.astype(jnp.bfloat16)[None],
        d_gain,
    )


def solution(mesh):
    placed = (
        P("replica", ("section", "tensor"), None),
        P("replica", None),
        P("replica", "section", None, "tensor"),
        P("replica", "section", None, "tensor"),
        P("replica", "section", None, "tensor"),
        P("replica", "section", None, "tensor"),
        P("replica"),
        P("replica"),
    )
    return jax.shard_map(
        local,
        mesh=mesh,
        in_specs=placed,
        out_specs=(
            P("replica", "section", None, "tensor"),
            P("section", "replica", "tensor"),
            P("section", "replica", "tensor"),
            P("replica", ("section", "tensor"), None),
            P(),
        ),
        check_vma=False,
    )
```

profile of v0, /device:TPU:1, one launch (start us, length us, event | category | flops | bytes accessed | tf_op | source)
XLA Modules:
  0.0 672.0 jit_solution(12037121111788663499)
XLA Ops:
  7.2 0.0 all-gather.2.cloned.1.call-start
  7.2 1.0 fusion.31
  8.2 0.7 mul.78
  9.0 1.6 multiply_convert_fusion.1
  10.5 0.0 all-gather.2.cloned.1.call-update
  10.5 0.0 reduce-scatter.3.cloned.1.call-start
  11.9 1.1 copy.49
  13.0 1.1 copy.48
  14.1 185.8 %all-gather.2.cloned.1.call-done = bf16[512,4096]{1,0:T(8,128)(2,1)} async-done(((bf16[8,4096]{1,0:T(8,128)(2,1)}), bf16[512,4096]{1,0:T(8,128)(2,1)}) %all-gather.2.cloned.1.call-update) | async-done | bytes 4194320 | tf_op jit(solution)/shard_map/all_gather | solution.py:56
  199.9 5.8 fusion.15
  205.7 0.6 fusion.41
  206.3 0.0 copy-start
  206.3 0.3 convolution_convert_fusion.1
  206.7 1.8 copy-done
  208.5 4.6 fusion.18
  213.1 0.4 multiply_reduce_fusion
  213.5 0.2 multiply_convert_fusion
  213.6 0.3 fusion.22
  214.0 0.2 copy.37
  214.2 10.0 %convolution_convert_fusion = bf16[4096,1024]{1,0:T(8,128)(2,1)} fusion(bf16[512,4096]{1,0:T(8,128)(2,1)} %all-gather.2.cloned.1.call-done, bf16[512,512]{0,1:T(8,128)(2,1)S(1)} %bitcast.77, bf16[512,512]{0,1:T(8,128)(2,1)S(1)} %bitcast.70), kind=kOutput, calls=%fused_computation.1 | convolution fusion | flops 4301258752 | bytes 13631488 | tf_op jit(solution)/shard_map/dot_general | solution.py:68
  224.2 0.0 reduce-scatter.3.cloned.1.call-update
  224.2 0.2 reduce-scatter.5.cloned.1.call-start
  224.5 0.0 copy-start.1
  224.5 4.8 fusion.4
  229.2 0.0 copy-done.1
  229.3 5.6 convolution_add_fusion
  234.9 0.0 reduce-scatter.5.cloned.1.call-update
  234.9 0.3 fusion.23
  235.2 0.8 copy.39
  236.1 75.7 %reduce-scatter.3.cloned.1.call-done = bf16[1024,1024]{1,0:T(8,128)(2,1)} async-done(((bf16[4096,1024]{1,0:T(8,128)(2,1)}), bf16[1024,1024]{1,0:T(8,128)(2,1)}) %reduce-scatter.3.cloned.1.call-update) | async-done | bytes 2097168 | tf_op jit(solution)/shard_map/reduce_scatter | solution.py:71
  311.8 2.0 convert_element_type.93
  313.8 0.0 copy-start.2
  313.8 1.9 fusion.25
  315.7 267.3 %reduce-scatter.5.cloned.1.call-done = f32[8,4096]{1,0:T(8,128)} async-done(((f32[512,4096]{1,0:T(8,128)}), f32[8,4096]{1,0:T(8,128)}) %reduce-scatter.5.cloned.1.call-update) | async-done | bytes 131088 | tf_op jit(solution)/shard_map/reduce_scatter | solution.py:78
  583.1 0.0 copy-done.2
  583.1 1.1 multiply_reduce_fusion.1
  584.2 79.0 %psum.7 = f32[4096]{0:T(1024)S(1)} all-reduce(f32[4096]{0:T(1024)S(1)} %get-tuple-element.15), channel_id=1, replica_groups=mesh['replica'=4,'section'=16,'tensor'=4] {'replica','section','tensor'}, use_global_device_ids=true, to_apply=%region_8.9 | all-reduce | flops 4096 | bytes 32768 | tf_op jit(solution)/shard_map/psum | solution.py:85
  663.2 0.6 broadcast_multiply_fusion
  663.8 1.6 fusion.34
  (4 shorter events, 0.0 us)
Async XLA Ops:
  7.2 192.7 %all-gather.2.cloned.1.call-start = ((), (), s32[]{:S(2)}) async-start(), calls=%async_computation.2 | async-start | bytes 4259840 | tf_op jit(solution)/shard_map/all_gather | solution.py:56
  10.5 301.2 %reduce-scatter.3.cloned.1.call-start = ((), (), s32[]{:S(2)}) async-start(), calls=%async_computation.3 | async-start | bytes 10485760 | tf_op jit(solution)/shard_map/reduce_scatter | solution.py:71
  206.3 2.2 copy-start
  224.2 358.9 %reduce-scatter.5.cloned.1.call-start = ((), (), s32[]{:S(2)}) async-start(), calls=%async_computation.4 | async-start | bytes 8519680 | tf_op jit(solution)/shard_map/reduce_scatter | solution.py:78
  224.5 4.8 copy-start.1
  313.8 269.3 %copy-start.2 = (bf16[1,8,4096]{2,1,0:T(8,128)(2,1)S(1)}, bf16[1,8,4096]{2,1,0:T(8,128)(2,1)}, u32[]{:S(2)}) copy-start(bf16[1,8,4096]{2,1,0:T(8,128)(2,1)} %param.8) | copy-start | bytes 196612
Sparse Core Ops, SparseCore 0:
  10.7 189.1 all-gather.1
  224.3 87.3 reduce-scatter.2
  314.3 268.7 reduce-scatter.4
where the time goes:
time: 673 us; the launch traced here: 672 us
  waiting for transfers between devices  529 us (79%)
  blocking collectives  79 us (12%)
  matrix products  32.7 us (5%)
  between operations  15.2 us (2%)
  other arithmetic  10.8 us (2%)
    reduce_scatter x1, waiting for transfers between devices, local(): lax.psum_scatter(term + lax.dot_general(d_value, w_value, contract_cols,...  267 us
    all_gather x1, waiting for transfers between devices, local(): lax.all_gather(normalized_hidden, ('section', 'tensor'), axis=0, tiled=True)  186 us
    psum x1, blocking collectives, local(): lax.psum(gain_gradient_terms, ('replica', 'section', 'tensor')) / replicas  79 us
    reduce_scatter x1, waiting for transfers between devices, local(): lax.psum_scatter(full_grads.astype(jnp.bfloat16), 'replica', scatter_dime...  75.7 us
  transfers between devices with their start and end apart: 3, of which 3 were waited for; matrix products, arithmetic and copies ran while one was open for 3% of the time, Pallas kernels for 0%

commit v1 on v0

v1 whole, which is shorter than its diff:
```python
import jax
import jax.numpy as jnp
from jax import lax
from jax.experimental import pallas as pl
from jax.experimental.pallas import tpu as pltpu
from jax.sharding import PartitionSpec as P

MESH = pl.DeviceIdType.MESH
F32 = jnp.float32
BF16 = jnp.bfloat16
D = 4096
ROWS = 512
DEC = 256
HD = 256
WID = 512
NX, NY, NZ = 4, 4, 8
QC = D // 4
EC = QC // 4
NSEM = 224


def dot(a, b, ca=1, cb=0):
    return lax.dot_general(a, b, (((ca,), (cb,)), ((), ())), preferred_element_type=F32)


def kernel(
    hid_ref, gain_ref, kw_ref, vw_ref, q_ref, ct_ref, elen_ref, dlen_ref,
    dq_ref, dwk_ref, dwv_ref, hg_ref, dg_ref,
    wk, wv, wsem, n32, x32, own16, G, E, acc, keys, vals, probs, grad, dsc, Dv, Dk,
    Ts, Tr, To, ry, rz, sy, sz, fin, dn, accv, acck,
    gp, gr, gz, gyx, gf, ssem, rsem,
):
    x = lax.axis_index("replica")
    sec = lax.axis_index("section")
    zlo = lax.axis_index("tensor")
    c = lax.rem(sec, 2)
    y = lax.rem(lax.div(sec, 2), NY)
    z = lax.div(sec, 2 * NY) * 4 + zlo
    sib = 1 - c

    def dev(dx=0, dy=0, dz=0, core=None):
        xx = lax.rem(x + dx + NX, NX)
        yy = lax.rem(y + dy + NY, NY)
        zz = lax.rem(z + dz + NZ, NZ)
        cc = c if core is None else core
        return (xx, (lax.div(zz, 4) * NY + yy) * 2 + cc, lax.rem(zz, 4))

    def yo(d):
        return lax.rem(y + d + NY, NY)

    def zo(d):
        return lax.rem(z + d + NZ, NZ)

    sibling = dev(core=sib)
    count = [0]
    sends = []

    def put(src, dst, to):
        i = count[0]
        count[0] += 1
        cp = pltpu.make_async_remote_copy(
            src_ref=src, dst_ref=dst, send_sem=ssem.at[i], recv_sem=rsem.at[i],
            device_id=to, device_id_type=MESH,
        )
        cp.start()
        sends.append(cp)
        return i

    def got(i, region):
        pltpu.make_async_remote_copy(
            src_ref=region, dst_ref=region, send_sem=ssem.at[i], recv_sem=rsem.at[i],
            device_id=sibling, device_id_type=MESH,
        ).wait_recv()

    background = []

    def poll(n=1):
        for _ in range(n):
            for g in list(background):
                if next(g, "end") == "end":
                    background.remove(g)

    def drain():
        while background:
            poll()

    wcopies = [
        pltpu.make_async_copy(kw_ref, wk, wsem.at[0]),
        pltpu.make_async_copy(vw_ref, wv, wsem.at[1]),
    ]
    for w in wcopies:
        w.start()

    partners = [sibling]
    partners += [dev(dz=d) for d in range(1, NZ)]
    partners += [dev(dx=a, dy=b) for a in range(NX) for b in range(NY) if (a, b) != (0, 0)]
    barrier = pltpu.get_barrier_semaphore()
    for p in partners:
        pl.semaphore_signal(barrier, inc=1, device_id=p, device_id_type=MESH)

    hid = hid_ref[...].astype(F32)
    gain = gain_ref[...].astype(F32)
    rms = jnp.sqrt(jnp.mean(hid * hid, axis=-1, keepdims=True) + 1e-06)
    xhat = hid / rms
    n32[...] = (xhat * gain).astype(BF16).astype(F32)
    pl.semaphore_wait(barrier, len(partners))

    i = put(n32, x32, sibling)
    got(i, x32)
    first = jnp.where(c == 0, n32[...], x32[...])
    second = jnp.where(c == 0, x32[...], n32[...])
    chip = jnp.concatenate([first, second], axis=0).astype(BF16)
    for q in range(4):
        own16[q] = chip[:, q * QC:(q + 1) * QC]
    G[2 * c, y, z] = own16[2 * c]
    G[2 * c + 1, y, z] = own16[2 * c + 1]

    def gather8(full, half, landed):
        a = put(full(z), full(z), dev(dz=1))
        b = put(full(z), full(z), dev(dz=-1))
        for k in (1, 2, 3):
            yield
            left, right = zo(-k), zo(k)
            got(a, full(left))
            if k < 3:
                a = put(full(left), full(left), dev(dz=1))
            else:
                a = put(half(left, 0), half(left, 0), dev(dz=1))
            got(b, full(right))
            if k < 3:
                b = put(full(right), full(right), dev(dz=-1))
            else:
                b = put(half(right, 1), half(right, 1), dev(dz=-1))
            landed(left)
            landed(right)
        yield
        far = zo(4)
        got(a, half(far, 0))
        got(b, half(far, 1))
        landed(far)

    def gather4(half, landed, mine, back, ahead, dst):
        a0 = put(half(mine, 0), half(mine, 0), dst(1))
        b1 = put(half(mine, 1), half(mine, 1), dst(-1))
        a1 = put(half(mine, 1), half(mine, 1), dst(1))
        b0 = put(half(mine, 0), half(mine, 0), dst(-1))
        yield
        got(a0, half(back(1), 0))
        f0 = put(half(back(1), 0), half(back(1), 0), dst(1))
        got(b1, half(ahead(1), 1))
        f1 = put(half(ahead(1), 1), half(ahead(1), 1), dst(-1))
        yield
        got(a1, half(back(1), 1))
        landed(back(1))
        got(b0, half(ahead(1), 0))
        landed(ahead(1))
        yield
        got(f0, half(ahead(2), 0))
        got(f1, half(ahead(2), 1))
        landed(ahead(2))

    def plane_gather(buf, lead, width, arrivals):
        pre = (slice(None),) * lead
        hw = width // 2
        lanes = (pl.ds(0, hw), pl.ds(hw, hw))

        def forward(region):
            i = put(region(c), region(c), sibling)
            arrivals.append((i, region(sib)))

        def first_z():
            def full(zz):
                return buf.at[(2 * c,) + pre + (y, zz)]

            def half(zz, h):
                return buf.at[(2 * c,) + pre + (y, zz, slice(None), lanes[h])]

            yield from gather8(full, half, lambda zz: None)
            forward(lambda cc: buf.at[(2 * cc,) + pre + (y,)])

            def yhalf(yy, h):
                return buf.at[(2 * c,) + pre + (yy, pl.ds(4 * h, 4))]

            def landed(yy):
                forward(lambda cc: buf.at[(2 * cc,) + pre + (yy,)])

            yield from gather4(
                yhalf, landed, y, lambda d: yo(-d), yo, lambda d: dev(dy=d)
            )

        def first_y():
            def half(yy, h):
                return buf.at[(2 * c + 1,) + pre + (yy, z, slice(None), lanes[h])]

            yield from gather4(
                half, lambda yy: None, y, lambda d: yo(-d), yo, lambda d: dev(dy=d)
            )

            def full(zz):
                return buf.at[(2 * c + 1,) + pre + (slice(None), zz)]

            def zhalf(zz, h):
                return buf.at[(2 * c + 1,) + pre + (pl.ds(2 * h, 2), zz)]

            def landed(zz):
                forward(lambda cc: buf.at[(2 * cc + 1,) + pre + (slice(None), zz)])

            landed(z)
            yield from gather8(full, zhalf, landed)

        return [first_z(), first_y()]

    g_arrivals = []
    background += plane_gather(G, 0, QC, g_arrivals)
    poll()
    extra = []
    for k in (1, 2, 3):
        to = lax.rem(x - k + NX, NX)
        for h in range(2):
            lane = pl.multiple_of((2 * c + h) * EC, EC)
            src = own16.at[to, :, pl.ds(lane, EC)]
            slot = E.at[2 * c + h, k - 1, y, z]
            extra.append((put(src, slot, dev(dx=-k)), slot))
    drain()

    for i, region in extra:
        got(i, region)
    e_arrivals = []
    background += plane_gather(E, 1, EC, e_arrivals)
    poll()

    def project(w, out, first):
        for j in range(4):
            if first and j == 2:
                for i, region in g_arrivals:
                    got(i, region)
            q = lax.rem(2 * c + j, 4)
            g = G[q].reshape(ROWS, QC)
            part = dot(g, w[pl.ds(pl.multiple_of(q * QC, QC), QC), :])
            if j == 0:
                acc[...] = part
            elif j < 3:
                acc[...] += part
            else:
                out[...] = (acc[...] + part).astype(BF16)
            if j % 2 == 1:
                poll()

    scale = HD ** (-0.5)
    wcopies[0].wait()
    project(wk, keys, True)

    row = lax.broadcasted_iota(jnp.int32, (ROWS, 1), 0)
    inner = row & 7
    rc = (row >> 3) & 1
    rz_ = (row >> 4) & 7
    ry_ = row >> 7
    pos = ((((rz_ >> 2) * NY + ry_) * 2 + rc) * 4 + (rz_ & 3)) * 8 + inner
    keep = pos < elen_ref[0]
    live = lax.broadcasted_iota(jnp.int32, (DEC, 1), 0) < dlen_ref[0]
    grad[...] = jnp.where(live, ct_ref[...], jnp.zeros((DEC, WID), BF16))
    for h in range(2):
        cols = slice(h * HD, (h + 1) * HD)
        s = dot(keys[:, cols], q_ref[:, cols], 1, 1) * scale
        s = jnp.where(keep, s, -1e30)
        top = jnp.max(s, axis=0, keepdims=True)
        e = jnp.where(keep, jnp.exp(s - top), 0.0)
        p = e / jnp.sum(e, axis=0, keepdims=True)
        probs[h] = p
        Dv[0, :, cols] = dot(p.astype(BF16), grad[:, cols]).astype(BF16)

    def along_x(buf):
        def at(slot, h):
            return buf.at[slot, pl.ds(h * (ROWS // 2), ROWS // 2)]

        a0 = put(at(0, 0), at(3, 0), dev(dx=1))
        b1 = put(at(0, 1), at(1, 1), dev(dx=-1))
        a1 = put(at(0, 1), at(3, 1), dev(dx=1))
        b0 = put(at(0, 0), at(1, 0), dev(dx=-1))
        yield
        got(a0, at(3, 0))
        f0 = put(at(3, 0), at(2, 0), dev(dx=1))
        got(b1, at(1, 1))
        f1 = put(at(1, 1), at(2, 1), dev(dx=-1))
        yield
        got(a1, at(3, 1))
        got(b0, at(1, 0))
        yield
        got(f0, at(2, 0))
        got(f1, at(2, 1))

    xv = along_x(Dv)
    next(xv)
    wcopies[1].wait()
    project(wv, vals, False)
    for h in range(2):
        cols = slice(h * HD, (h + 1) * HD)
        dp = dot(vals[:, cols], grad[:, cols], 1, 1)
        p = probs[h]
        ds = (p * (dp - jnp.sum(p * dp, axis=0, keepdims=True))).astype(BF16)
        dsc[h] = ds
        Dk[0, :, cols] = (dot(ds, q_ref[:, cols]) * scale).astype(BF16)
    xk = along_x(Dk)
    next(xk)

    t_in = []
    for j in range(4):
        q = lax.rem(2 * sib + j, 4)
        w = pl.ds(pl.multiple_of(q * QC, QC), QC)
        t = dot(Dk[0], wk[w, :], 1, 1) + dot(Dv[0], wv[w, :], 1, 1)
        if j < 2:
            Ts[j] = t.astype(BF16).reshape(NY, NZ, 16, QC)
            t_in.append(put(Ts.at[j], Tr.at[j], sibling))
        else:
            To[j - 2] = t.reshape(NY, NZ, 16, QC)
        poll()
    next(xv, None)

    def sum4(own, stage, land, base, dst, put_result, mine, off):
        def send(slot, value, to):
            stage[base + slot] = value.astype(BF16)
            return put(stage.at[base + slot], land.at[base + slot], to)

        a0 = send(0, own(off(2), 0), dst(1))
        b1 = send(1, own(off(2), 1), dst(-1))
        a1 = send(2, own(off(1), 1), dst(1))
        b0 = send(3, own(off(-1), 0), dst(-1))
        yield
        got(a0, land.at[base])
        f0 = send(4, own(off(1), 0) + land[base].astype(F32), dst(1))
        got(b1, land.at[base + 1])
        f1 = send(5, own(off(-1), 1) + land[base + 1].astype(F32), dst(-1))
        yield
        got(a1, land.at[base + 2])
        got(b0, land.at[base + 3])
        yield
        got(f0, land.at[base + 4])
        got(f1, land.at[base + 5])
        put_result(0, own(mine, 0) + land[base + 3].astype(F32) + land[base + 4].astype(F32))
        put_result(1, own(mine, 1) + land[base + 2].astype(F32) + land[base + 5].astype(F32))

    def sum8(own, stage, land, put_result):
        stage[0, 0] = own(zo(4), 0).astype(BF16)
        a = put(stage.at[0, 0], land.at[0, 0], dev(dz=1))
        stage[4, 1] = own(zo(4), 1).astype(BF16)
        b = put(stage.at[4, 1], land.at[4, 1], dev(dz=-1))
        for s, k in ((1, 3), (2, 2), (3, 1)):
            yield
            if s == 1:
                got(a, land.at[0, 0])
            else:
                got(a, land.at[s - 1])
            for h in range(2):
                v = own(zo(k), h)
                if s > 1 or h == 0:
                    v = v + land[s - 1, h].astype(F32)
                stage[s, h] = v.astype(BF16)
            a = put(stage.at[s], land.at[s], dev(dz=1))
            if s == 1:
                got(b, land.at[4, 1])
            else:
                got(b, land.at[3 + s])
            for h in range(2):
                v = own(zo(-k), h)
                if s > 1 or h == 1:
                    v = v + land[3 + s, h].astype(F32)
                stage[4 + s, h] = v.astype(BF16)
            b = put(stage.at[4 + s], land.at[4 + s], dev(dz=-1))
        yield
        got(a, land.at[3])
        got(b, land.at[7])
        for h in range(2):
            put_result(h, own(z, h) + land[3, h].astype(F32) + land[7, h].astype(F32))

    hq = QC // 2
    lanes = (slice(0, hq), slice(hq, QC))

    def sum_y_first():
        got(t_in[0], Tr.at[0])
        To[0] += Tr[0].astype(F32)

        def own(yy, h):
            return To[0, yy, 4 * h:4 * h + 4]

        def result(h, v):
            To[0, y, 4 * h:4 * h + 4] = v

        yield from sum4(own, sy[0], ry[0], 0, lambda d: dev(dy=d), result, y, yo)

        def own2(zz, h):
            return To[0, y, zz, :, lanes[h]]

        def result2(h, v):
            fin[0, :, :, lanes[h]] = v.reshape(2, 8, hq)

        yield from sum8(own2, sz[0], rz[0], result2)

    def sum_z_first():
        got(t_in[1], Tr.at[1])
        To[1] += Tr[1].astype(F32)

        def own(zz, h):
            return To[1, 2 * h:2 * h + 2, zz]

        def result(h, v):
            To[1, 2 * h:2 * h + 2, z] = v

        yield from sum8(own, sz[1], rz[1], result)

        def own2(yy, h):
            return To[1, yy, z, :, lanes[h]]

        def result2(h, v):
            fin[1, :, :, lanes[h]] = v.reshape(2, 8, hq)

        yield from sum4(own2, sy[1], ry[1], 0, lambda d: dev(dy=d), result2, y, yo)

    drain()
    for i, region in e_arrivals:
        got(i, region)

    def weight_part(buf, total, out, k):
        for q in range(4):
            r = slice(q * EC, (q + 1) * EC)
            if k == 0:
                total[r, :] = dot(G[x].reshape(ROWS, QC)[:, r], buf[0], 0, 0)
            else:
                part = dot(E[q, k - 1].reshape(ROWS, EC), buf[k], 0, 0)
                if k == 2:
                    out[r, :] = ((total[r, :] + part) / NX).astype(BF16)
                else:
                    total[r, :] += part

    def queries():
        for h in range(2):
            cols = slice(h * HD, (h + 1) * HD)
            dq_ref[:, cols] = (dot(dsc[h], keys[:, cols], 0, 0) * scale).astype(BF16)

    background += [sum_y_first(), sum_z_first()]
    poll()
    queries()
    poll()
    weight_part(Dv, accv, dwv_ref, 0)
    poll()
    weight_part(Dk, acck, dwk_ref, 0)
    poll()
    next(xv, None)
    weight_part(Dv, accv, dwv_ref, 1)
    poll()
    next(xv, None)
    weight_part(Dv, accv, dwv_ref, 3)
    poll()
    drain()

    i = put(fin.at[:, sib], dn, sibling)
    got(i, dn)
    own_half = jnp.concatenate([fin[0, c], fin[1, c]], axis=1)
    other = jnp.concatenate([dn[0], dn[1]], axis=1)
    dnorm = jnp.concatenate(
        [jnp.where(c == 0, own_half, other), jnp.where(c == 0, other, own_half)], axis=1
    )
    terms = jnp.sum(dnorm * xhat, axis=0, keepdims=True)
    for j in range(8):
        for h in range(2):
            lo = j * 512 + h * 256
            gp[h, j:j + 1, :] = terms[:, lo:lo + 256]
    i1 = put(gp.at[sib], gr, sibling)
    scaled = gain * dnorm
    hg = (scaled - xhat * jnp.mean(scaled * xhat, axis=-1, keepdims=True)) / rms
    hg_ref[...] = hg.astype(BF16)
    got(i1, gr)
    gz[z] = gp[c] + gr[...]
    idx = [put(gz.at[z], gz.at[z], dev(dz=d)) for d in range(1, NZ)]
    next(xk, None)
    for d, i in zip(range(1, NZ), idx):
        got(i, gz.at[zo(-d)])
    slot = y * NX + x
    gyx[slot] = jnp.sum(gz[...], axis=0)
    idx = []
    for a in range(NX):
        for b in range(NY):
            if (a, b) != (0, 0):
                i = put(gyx.at[slot], gyx.at[slot], dev(dx=a, dy=b))
                idx.append((i, yo(-b) * NX + lax.rem(x - a + NX, NX)))
    for i, s in idx:
        got(i, gyx.at[s])
    gf[c] = jnp.sum(gyx[...], axis=0) / NX
    i2 = put(gf.at[c], gf.at[c], sibling)

    next(xv, None)
    weight_part(Dv, accv, dwv_ref, 2)
    next(xk, None)
    weight_part(Dk, acck, dwk_ref, 1)
    weight_part(Dk, acck, dwk_ref, 3)
    got(i2, gf.at[sib])
    for j in range(8):
        for h in range(2):
            lo = j * 512 + h * 256
            dg_ref[0:1, lo:lo + 256] = gf[h, j:j + 1, :]
    next(xk, None)
    weight_part(Dk, acck, dwk_ref, 2)
    for cp in sends:
        cp.wait_send()
    assert count[0] <= NSEM, count[0]


def local(enc_hidden, enc_gain, key_weight, value_weight, queries, cotangent, enc_len, dec_len):
    vmem = pl.BlockSpec(memory_space=pltpu.VMEM)
    hbm = pl.BlockSpec(memory_space=pl.ANY)
    smem = pl.BlockSpec(memory_space=pltpu.SMEM)
    v = pltpu.VMEM
    outs = pl.pallas_call(
        kernel,
        out_shape=(
            jax.ShapeDtypeStruct((DEC, WID), BF16),
            jax.ShapeDtypeStruct((QC, WID), BF16),
            jax.ShapeDtypeStruct((QC, WID), BF16),
            jax.ShapeDtypeStruct((8, D), BF16),
            jax.ShapeDtypeStruct((1, D), F32),
        ),
        in_specs=[vmem, vmem, hbm, hbm, vmem, vmem, smem, smem],
        out_specs=(vmem,) * 5,
        scratch_shapes=[
            v((D, WID), BF16),
            v((D, WID), BF16),
            pltpu.SemaphoreType.DMA((2,)),
            v((8, D), F32),
            v((8, D), F32),
            v((4, 16, QC), BF16),
            v((4, NY, NZ, 16, QC), BF16),
            v((4, 3, NY, NZ, 16, EC), BF16),
            v((ROWS, WID), F32),
            v((ROWS, WID), BF16),
            v((ROWS, WID), BF16),
            v((2, ROWS, DEC), F32),
            v((DEC, WID), BF16),
            v((2, ROWS, DEC), BF16),
            v((4, ROWS, WID), BF16),
            v((4, ROWS, WID), BF16),
            v((2, NY, NZ, 16, QC), BF16),
            v((2, NY, NZ, 16, QC), BF16),
            v((2, NY, NZ, 16, QC), F32),
            [v((6, 4, 16, QC), BF16), v((6, 16, QC // 2), BF16)],
            [v((8, 2, 16, QC // 2), BF16), v((8, 2, 2, 16, QC), BF16)],
            [v((6, 4, 16, QC), BF16), v((6, 16, QC // 2), BF16)],
            [v((8, 2, 16, QC // 2), BF16), v((8, 2, 2, 16, QC), BF16)],
            v((2, 2, 8, QC), F32),
            v((2, 8, QC), F32),
            v((QC, WID), F32),
            v((QC, WID), F32),
            v((2, 8, 256), F32),
            v((8, 256), F32),
            v((NZ, 8, 256), F32),
            v((NX * NY, 8, 256), F32),
            v((2, 8, 256), F32),
            pltpu.SemaphoreType.DMA((NSEM,)),
            pltpu.SemaphoreType.DMA((NSEM,)),
        ],
        compiler_params=pltpu.CompilerParams(
            collective_id=0, has_side_effects=True, vmem_limit_bytes=60 * 1024 * 1024
        ),
        cost_estimate=pl.CostEstimate(
            flops=15_000_000_000, bytes_accessed=12_000_000, transcendentals=300_000
        ),
    )(
        enc_hidden[0], enc_gain, key_weight[0, 0], value_weight[0, 0],
        queries[0, 0], cotangent[0, 0], enc_len, dec_len,
    )
    dq, dwk, dwv, hg, dg = outs
    return dq[None, None], dwk[None], dwv[None], hg[None], dg[0]


def solution(mesh):
    placed = (
        P("replica", ("section", "tensor"), None),
        P("replica", None),
        P("replica", "section", None, "tensor"),
        P("replica", "section", None, "tensor"),
        P("replica", "section", None, "tensor"),
        P("replica", "section", None, "tensor"),
        P("replica"),
        P("replica"),
    )
    return jax.shard_map(
        local,
        mesh=mesh,
        in_specs=placed,
        out_specs=(
            P("replica", "section", None, "tensor"),
            P("section", "replica", "tensor"),
            P("section", "replica", "tensor"),
            P("replica", ("section", "tensor"), None),
            P(),
        ),
        check_vma=False,
    )
```

time: 673 us -> 126 us (0.19)
  waiting for transfers between devices: 529 us -> 0 us
  Pallas kernels: 0 us -> 116 us
  blocking collectives: 79 us -> 0 us
  matrix products: 32.7 us -> 0 us
  between operations: 15.2 us -> 1.95 us
  other arithmetic: 10.8 us -> 0 us
    reduce_scatter x2 -> x0, waiting for transfers between devices: 343 us -> none  [the longest x1 267 us: local(): lax.psum_scatter(term + lax.dot_general(d_value, w_value, contract_cols,...]
    all_gather x1 -> x0, waiting for transfers between devices: 186 us -> none  [local(): lax.all_gather(normalized_hidden, ('section', 'tensor'), axis=0, tiled=True)]
    pallas_call x0 -> x1, Pallas kernels: none -> 116 us  [local(): pl.pallas_call(kernel, out_shape=(jax.ShapeDtypeStruct((DEC, WID), BF16),...]
    psum x1 -> x0, blocking collectives: 79 us -> none  [local(): lax.psum(gain_gradient_terms, ('replica', 'section', 'tensor')) / replicas]
    dot_general x9 -> x0, matrix products: 32.1 us -> none  [the longest x1 10 us: local(): lax.dot_general(whole, both_grads, contract_rows, preferred_element_type=...]
  transfers between devices with their start and end apart: 3 -> 0, of which waited for: 3 -> 0; matrix products, arithmetic and copies ran while one was open for 3% -> 0% of each run, Pallas kernels for 0% -> 0%
where the time goes in v1:
time: 126 us
  Pallas kernels  116 us (92%)
  local copies, waits for them, and re-layouts  7.47 us (6%)
  between operations  1.95 us (2%)
    pallas_call x1, Pallas kernels, local(): pl.pallas_call(kernel, out_shape=(jax.ShapeDtypeStruct((DEC, WID), BF16),...  116 us
    unnamed x9, local copies, waits for them, and re-layouts  7.47 us

profile of v1, /device:TPU:1, one launch (start us, length us, event | category | flops | bytes accessed | tf_op | source)
XLA Modules:
  0.0 125.8 jit_solution(13128547115391370862)
XLA Ops:
  1.9 116.4 %shard_map.119 = (bf16[256,512]{1,0:T(8,128)(2,1)}, bf16[1024,512]{1,0:T(8,128)(2,1)}, bf16[1024,512]{1,0:T(8,128)(2,1)}, bf16[8,4096]{1,0:T(8,128)(2,1)}, f32[1,4096]{1,0:T(1,128)}) custom-call(bf16[8,4096]{1,0:T(8,128)(2,1)} %bitcast.19, bf16[1,4096]{1,0:T(2,128)(2,1)} %gain_ref.1, bf16[4096,512]{1,0:T(8,128)(2,1)} %bitcast.15, ...), custom_call_target="tpu_custom_call" | custom-call | flops 15000000512 | bytes 12000000 | tf_op jit(solution)/shard_map/pallas_call | solution.py:512
  118.3 0.0 copy-start
  118.3 0.0 copy-start.1
  118.3 1.7 %copy.20 = bf16[1,1,256,512]{3,2,1,0:T(8,128)(2,1)} copy(bf16[1,1,256,512]{3,2,1,0:T(8,128)(2,1)} %bitcast.12) | data formatting | bytes 524288
  120.0 2.3 %copy.21 = bf16[1,1024,512]{2,1,0:T(8,128)(2,1)} copy(bf16[1,1024,512]{2,1,0:T(8,128)(2,1)} %bitcast.11) | data formatting | bytes 2097152
  122.3 2.3 %copy.22 = bf16[1,1024,512]{2,1,0:T(8,128)(2,1)} copy(bf16[1,1024,512]{2,1,0:T(8,128)(2,1)} %bitcast.10) | data formatting | bytes 2097152
  124.5 0.0 copy-done
  124.5 0.6 copy.23
  125.2 0.0 copy-done.1
  125.2 0.6 copy.24
Async XLA Ops:
  118.3 6.2 %copy-start = (bf16[8,4096]{1,0:T(8,128)(2,1)S(1)}, bf16[8,4096]{1,0:T(8,128)(2,1)}, u32[]{:S(2)}) copy-start(bf16[8,4096]{1,0:T(8,128)(2,1)} %get-tuple-element.13) | copy-start | bytes 196612
  118.3 6.9 %copy-start.1 = (f32[1,4096]{1,0:T(1,128)S(1)}, f32[1,4096]{1,0:T(1,128)}, u32[]{:S(2)}) copy-start(f32[1,4096]{1,0:T(1,128)} %get-tuple-element.14) | copy-start | bytes 49156

commit v2 on v1

v2 whole, which is shorter than its diff:
```python
import jax
import jax.numpy as jnp
from jax import lax
from jax.experimental import pallas as pl
from jax.experimental.pallas import tpu as pltpu
from jax.sharding import PartitionSpec as P

MESH = pl.DeviceIdType.MESH
F32 = jnp.float32
BF16 = jnp.bfloat16
D = 4096
ROWS = 512
DEC = 256
HD = 256
WID = 512
NX, NY, NZ = 4, 4, 8
QC = D // 4
EC = QC // 4
NSEM = 96
NSEND = 48


def dot(a, b, ca=1, cb=0):
    return lax.dot_general(a, b, (((ca,), (cb,)), ((), ())), preferred_element_type=F32)


def kernel(
    hid_ref, gain_ref, kw_ref, vw_ref, q_ref, ct_ref, elen_ref, dlen_ref,
    dq_ref, dwk_ref, dwv_ref, hg_ref, dg_ref,
    wk, wv, wsem, n32, x32, G, E, acc, keys, vals, probs, grad, dsc, Dv, Dk,
    Ts, Tr, To, ly, lz, sy, sz, fin, dn, accv, acck,
    gz, gy, gx, gf, ssem, rsem, esend, erecv,
):
    x = lax.axis_index("replica")
    sec = lax.axis_index("section")
    zlo = lax.axis_index("tensor")
    c = lax.rem(sec, 2)
    y = lax.rem(lax.div(sec, 2), NY)
    z = lax.div(sec, 2 * NY) * 4 + zlo
    sib = 1 - c

    def dev(dx=0, dy=0, dz=0, core=None):
        xx = lax.rem(x + dx + NX, NX)
        yy = lax.rem(y + dy + NY, NY)
        zz = lax.rem(z + dz + NZ, NZ)
        cc = c if core is None else core
        return (xx, (lax.div(zz, 4) * NY + yy) * 2 + cc, lax.rem(zz, 4))

    def xo(d):
        return lax.rem(x + d + NX, NX)

    def yo(d):
        return lax.rem(y + d + NY, NY)

    def zo(d):
        return lax.rem(z + d + NZ, NZ)

    sibling = dev(core=sib)
    count = [0]
    sends = {}

    def put(src, dst, to):
        i = count[0]
        count[0] += 1
        s = i % NSEND
        if s in sends:
            sends[s].wait_send()
        cp = pltpu.make_async_remote_copy(
            src_ref=src, dst_ref=dst, send_sem=ssem.at[s], recv_sem=rsem.at[i],
            device_id=to, device_id_type=MESH,
        )
        cp.start()
        sends[s] = cp
        return i

    def got(i, region):
        pltpu.make_async_remote_copy(
            src_ref=region, dst_ref=region, send_sem=ssem.at[0], recv_sem=rsem.at[i],
            device_id=sibling, device_id_type=MESH,
        ).wait_recv()

    background = []

    def poll(n=1):
        for _ in range(n):
            for g in list(background):
                if next(g, "end") == "end":
                    background.remove(g)

    def drain():
        while background:
            poll()

    wcopies = [
        pltpu.make_async_copy(kw_ref, wk, wsem.at[0]),
        pltpu.make_async_copy(vw_ref, wv, wsem.at[1]),
    ]
    for w in wcopies:
        w.start()

    partners = [sibling]
    partners += [dev(dz=d) for d in range(1, NZ)]
    partners += [dev(dy=d) for d in range(1, NY)]
    partners += [dev(dx=d) for d in range(1, NX)]
    barrier = pltpu.get_barrier_semaphore()
    for p in partners:
        pl.semaphore_signal(barrier, inc=1, device_id=p, device_id_type=MESH)

    hid = hid_ref[...].astype(F32)
    gain = gain_ref[...].astype(F32)
    rms = jnp.sqrt(jnp.mean(hid * hid, axis=-1, keepdims=True) + 1e-06)
    xhat = hid / rms
    n32[...] = (xhat * gain).astype(BF16).astype(F32)
    pl.semaphore_wait(barrier, len(partners))

    hc = D // 2
    i = put(n32.at[:, pl.ds(pl.multiple_of(sib * hc, hc), hc)], x32, sibling)
    mine = jnp.where(c == 0, n32[:, :hc], n32[:, hc:])
    got(i, x32)
    other = x32[...]
    chip = jnp.concatenate(
        [jnp.where(c == 0, mine, other), jnp.where(c == 0, other, mine)], axis=0
    ).astype(BF16)
    for j in range(2):
        G[2 * c + j, y, z] = chip[:, j * QC:(j + 1) * QC]

    def ring8(half, landed):
        a = [put(half(z, h), half(z, h), dev(dz=1)) for h in (0, 1)]
        b = [put(half(z, h), half(z, h), dev(dz=-1)) for h in (1, 0)][::-1]
        for k in (1, 2, 3):
            yield
            left, right = zo(-k), zo(k)
            for far in (True, False):
                ha, hb = (0, 1) if far else (1, 0)
                got(a[ha], half(left, ha))
                if k < 3 or far:
                    a[ha] = put(half(left, ha), half(left, ha), dev(dz=1))
                got(b[hb], half(right, hb))
                if k < 3 or far:
                    b[hb] = put(half(right, hb), half(right, hb), dev(dz=-1))
            landed(left)
            landed(right)
        yield
        got(a[0], half(zo(4), 0))
        got(b[1], half(zo(4), 1))
        landed(zo(4))

    arrivals = []

    def forward(region):
        i = put(region(c), region(c), sibling)
        arrivals.append((i, region(sib)))

    def to_replica(j, at):
        q = 2 * c + j

        @pl.when(q != x)
        def _():
            slot = jnp.maximum(lax.rem(x - q + NX, NX) - 1, 0)
            pltpu.make_async_remote_copy(
                src_ref=G.at[(q,) + at], dst_ref=E.at[(slot,) + at],
                send_sem=esend.at[j], recv_sem=erecv.at[slot],
                device_id=dev(dx=q - x), device_id_type=MESH,
            ).start()

    every = slice(None)

    def gather_z_first():
        q = 2 * c
        order = (4, 3, 5, 2, 6, 1, 7)
        idx = [put(G.at[q, y, z], G.at[q, y, z], dev(dz=d)) for d in order]
        yield
        yield
        for d, i in zip(order, idx):
            got(i, G.at[q, y, zo(-d)])
        order = (2, 1, 3)
        idx = [put(G.at[q, y], G.at[q, y], dev(dy=d)) for d in order]
        forward(lambda cc: G.at[2 * cc, y])
        to_replica(0, (y,))
        yield
        yield
        for d, i in zip(order, idx):
            yy = yo(-d)
            got(i, G.at[q, yy])
            forward(lambda cc: G.at[2 * cc, yy])
            to_replica(0, (yy,))

    def gather_y_first():
        q = 2 * c + 1
        order = (2, 1, 3)
        idx = [put(G.at[q, y, z], G.at[q, y, z], dev(dy=d)) for d in order]
        yield
        for d, i in zip(order, idx):
            got(i, G.at[q, yo(-d), z])

        def half(zz, h):
            return G.at[q, pl.ds(2 * h, 2), zz]

        def landed(zz):
            forward(lambda cc: G.at[2 * cc + 1, :, zz])
            to_replica(1, (every, zz))

        first = ring8(half, landed)
        next(first)
        landed(z)
        yield
        yield from first

    background += [gather_y_first(), gather_z_first()]
    drain()

    def project(w, out, first):
        for j in range(4):
            if first and j == 2:
                for i, region in arrivals:
                    got(i, region)
            q = lax.rem(2 * c + j, 4)
            part = dot(G[q].reshape(ROWS, QC), w[pl.ds(pl.multiple_of(q * QC, QC), QC), :])
            if j == 0:
                acc[...] = part
            elif j < 3:
                acc[...] += part
            else:
                out[...] = (acc[...] + part).astype(BF16)

    scale = HD ** (-0.5)
    row = lax.broadcasted_iota(jnp.int32, (ROWS, 1), 0)
    inner = row & 7
    row_c = (row >> 3) & 1
    row_z = (row >> 4) & 7
    row_y = row >> 7
    pos = ((((row_z >> 2) * NY + row_y) * 2 + row_c) * 4 + (row_z & 3)) * 8 + inner
    keep = pos < elen_ref[0]
    live = lax.broadcasted_iota(jnp.int32, (DEC, 1), 0) < dlen_ref[0]
    grad[...] = jnp.where(live, ct_ref[...], jnp.zeros((DEC, WID), BF16))
    wcopies[0].wait()
    project(wk, keys, True)
    for h in range(2):
        cols = slice(h * HD, (h + 1) * HD)
        s = dot(keys[:, cols], q_ref[:, cols], 1, 1) * scale
        s = jnp.where(keep, s, -1e30)
        top = jnp.max(s, axis=0, keepdims=True)
        e = jnp.where(keep, jnp.exp(s - top), 0.0)
        p = e / jnp.sum(e, axis=0, keepdims=True)
        probs[h] = p
        Dv[0, :, cols] = dot(p.astype(BF16), grad[:, cols]).astype(BF16)

    def along_x(buf):
        def at(slot, h):
            return buf.at[slot, pl.ds(h * (ROWS // 2), ROWS // 2)]

        a0 = put(at(0, 0), at(3, 0), dev(dx=1))
        b1 = put(at(0, 1), at(1, 1), dev(dx=-1))
        a1 = put(at(0, 1), at(3, 1), dev(dx=1))
        b0 = put(at(0, 0), at(1, 0), dev(dx=-1))
        yield
        got(a0, at(3, 0))
        f0 = put(at(3, 0), at(2, 0), dev(dx=1))
        got(b1, at(1, 1))
        f1 = put(at(1, 1), at(2, 1), dev(dx=-1))
        yield
        got(a1, at(3, 1))
        got(b0, at(1, 0))
        yield
        got(f0, at(2, 0))
        got(f1, at(2, 1))

    xv = along_x(Dv)
    next(xv)
    wcopies[1].wait()
    project(wv, vals, False)
    for h in range(2):
        cols = slice(h * HD, (h + 1) * HD)
        dp = dot(vals[:, cols], grad[:, cols], 1, 1)
        p = probs[h]
        ds = (p * (dp - jnp.sum(p * dp, axis=0, keepdims=True))).astype(BF16)
        dsc[h] = ds
        Dk[0, :, cols] = (dot(ds, q_ref[:, cols]) * scale).astype(BF16)
    xk = along_x(Dk)
    next(xk)

    def sum_y_first():
        order = (2, 1, 3)
        idx = []
        for d in order:
            sy[0][d - 1] = To[0, yo(d)].astype(BF16)
            idx.append(put(sy[0].at[d - 1], ly[0].at[d - 1], dev(dy=d)))
        yield
        yield
        for d, i in zip(order, idx):
            got(i, ly[0].at[d - 1])
        v = To[0, y]
        for d in range(3):
            v = v + ly[0][d].astype(F32)
        To[0, y] = v
        order = (4, 3, 5, 2, 6, 1, 7)
        idx = []
        for d in order:
            sz[0][d - 1] = To[0, y, zo(d)].astype(BF16)
            idx.append(put(sz[0].at[d - 1], lz[0].at[d - 1], dev(dz=d)))
        yield
        yield
        for d, i in zip(order, idx):
            got(i, lz[0].at[d - 1])
        v = To[0, y, z]
        for d in range(7):
            v = v + lz[0][d].astype(F32)
        fin[0] = v.reshape(2, 8, QC)

    def sum_z_first():
        stage, land = sz[1], lz[1]

        def own(zz, h):
            return To[1, 2 * h:2 * h + 2, zz]

        def send(slot, h, value, to):
            stage[slot, h] = value.astype(BF16)
            return put(stage.at[slot, h], land.at[slot, h], to)

        a, b = [None, None], [None, None]
        a[0] = send(0, 0, own(zo(4), 0), dev(dz=1))
        b[1] = send(4, 1, own(zo(4), 1), dev(dz=-1))
        a[1] = send(1, 1, own(zo(3), 1), dev(dz=1))
        b[0] = send(5, 0, own(zo(-3), 0), dev(dz=-1))
        for s, k in ((1, 3), (2, 2), (3, 1)):
            yield
            for h in ((0, 1) if s > 1 else (0,)):
                got(a[h], land.at[s - 1, h])
                a[h] = send(s, h, own(zo(k), h) + land[s - 1, h].astype(F32), dev(dz=1))
                g = 1 - h
                got(b[g], land.at[3 + s, g])
                b[g] = send(4 + s, g, own(zo(-k), g) + land[3 + s, g].astype(F32), dev(dz=-1))
        yield
        for h in range(2):
            got(a[h], land.at[3, h])
            got(b[h], land.at[7, h])
            To[1, 2 * h:2 * h + 2, z] = (
                own(z, h) + land[3, h].astype(F32) + land[7, h].astype(F32)
            )
        order = (2, 1, 3)
        idx = []
        for d in order:
            sy[1][d - 1] = To[1, yo(d), z].astype(BF16)
            idx.append(put(sy[1].at[d - 1], ly[1].at[d - 1], dev(dy=d)))
        yield
        for d, i in zip(order, idx):
            got(i, ly[1].at[d - 1])
        v = To[1, y, z]
        for d in range(3):
            v = v + ly[1][d].astype(F32)
        fin[1] = v.reshape(2, 8, QC)

    t_in = []
    sums = [sum_y_first(), sum_z_first()]
    for j in range(4):
        q = lax.rem(2 * sib + j, 4)
        w = pl.ds(pl.multiple_of(q * QC, QC), QC)
        t = dot(Dk[0], wk[w, :], 1, 1) + dot(Dv[0], wv[w, :], 1, 1)
        if j < 2:
            Ts[j] = t.astype(BF16).reshape(NY, NZ, 16, QC)
            t_in.append(put(Ts.at[j], Tr.at[j], sibling))
        else:
            got(t_in[j - 2], Tr.at[j - 2])
            To[j - 2] = t.reshape(NY, NZ, 16, QC) + Tr[j - 2].astype(F32)
            next(sums[j - 2])
    next(xv)

    gsel = jnp.where(c == 0, gain[:, :hc], gain[:, hc:])
    for j in range(2):
        prod = To[j].reshape(ROWS, QC) * G[2 * c + j].reshape(ROWS, QC).astype(F32)
        terms = jnp.sum(prod, axis=0, keepdims=True) / gsel[:, j * QC:(j + 1) * QC]
        for r in range(4):
            gz[z, 4 * j + r:4 * j + r + 1, :] = terms[:, r * 256:(r + 1) * 256]

    def sum_gain():
        idx = [(put(gz.at[z], gz.at[z], dev(dz=d)), zo(-d)) for d in range(1, NZ)]
        yield
        for i, s in idx:
            got(i, gz.at[s])
        gy[y] = jnp.sum(gz[...], axis=0)
        idx = [(put(gy.at[y], gy.at[y], dev(dy=d)), yo(-d)) for d in range(1, NY)]
        yield
        for i, s in idx:
            got(i, gy.at[s])
        gx[x] = jnp.sum(gy[...], axis=0)
        idx = [(put(gx.at[x], gx.at[x], dev(dx=d)), xo(-d)) for d in range(1, NX)]
        yield
        for i, s in idx:
            got(i, gx.at[s])
        gf[c] = jnp.sum(gx[...], axis=0) / NX
        i = put(gf.at[c], gf.at[c], sibling)
        yield
        got(i, gf.at[sib])
        for h in range(2):
            for r in range(8):
                lo = h * hc + r * 256
                dg_ref[0:1, lo:lo + 256] = gf[h, r:r + 1, :]

    def weight_part(buf, total, out, k):
        src = G.at[x] if k == 0 else E.at[k - 1]
        for q in range(4):
            r = slice(q * EC, (q + 1) * EC)
            part = dot(src[:, :, :, r].reshape(ROWS, EC), buf[k], 0, 0)
            if k == 0:
                total[r, :] = part
            elif k == 2:
                out[r, :] = ((total[r, :] + part) / NX).astype(BF16)
            else:
                total[r, :] += part

    background += sums + [sum_gain()]
    poll()
    for h in range(2):
        cols = slice(h * HD, (h + 1) * HD)
        dq_ref[:, cols] = (dot(dsc[h], keys[:, cols], 0, 0) * scale).astype(BF16)
    weight_part(Dv, accv, dwv_ref, 0)
    poll()
    weight_part(Dk, acck, dwk_ref, 0)

    owner = lax.div(x, 2)
    handed = []
    for k in range(3):
        def piece(send, recv):
            return pltpu.make_async_remote_copy(
                src_ref=E.at[k], dst_ref=E.at[k], send_sem=esend.at[send],
                recv_sem=erecv.at[recv], device_id=sibling, device_id_type=MESH,
            )

        @pl.when(c == owner)
        def _():
            piece(2 + k, k).wait_recv()
            piece(2 + k, 3 + k).start()

        handed.append(piece(2 + k, 3 + k))
    poll()
    next(xv)
    for cp in handed:
        @pl.when(c != owner)
        def _():
            cp.wait_recv()
    weight_part(Dv, accv, dwv_ref, 1)
    weight_part(Dv, accv, dwv_ref, 3)
    poll()
    next(xk)
    next(xv, None)
    weight_part(Dv, accv, dwv_ref, 2)
    drain()

    i = put(fin.at[:, sib], dn, sibling)
    got(i, dn)
    own_half = jnp.concatenate([fin[0, c], fin[1, c]], axis=1)
    other_half = jnp.concatenate([dn[0], dn[1]], axis=1)
    dnorm = jnp.concatenate(
        [jnp.where(c == 0, own_half, other_half), jnp.where(c == 0, other_half, own_half)],
        axis=1,
    )
    scaled = gain * dnorm
    hg = (scaled - xhat * jnp.mean(scaled * xhat, axis=-1, keepdims=True)) / rms
    hg_ref[...] = hg.astype(BF16)

    next(xk)
    weight_part(Dk, acck, dwk_ref, 1)
    weight_part(Dk, acck, dwk_ref, 3)
    next(xk, None)
    weight_part(Dk, acck, dwk_ref, 2)
    for cp in sends.values():
        cp.wait_send()
    for j in range(2):
        @pl.when(2 * c + j != x)
        def _():
            pltpu.make_async_remote_copy(
                src_ref=G.at[2 * c + j], dst_ref=E.at[0], send_sem=esend.at[j],
                recv_sem=erecv.at[0], device_id=sibling, device_id_type=MESH,
            ).wait_send()
    for cp in handed:
        @pl.when(c == owner)
        def _():
            cp.wait_send()
    assert count[0] == NSEM, count[0]


def place(dq, dwk, dwv, hg, dg, dq_out, dwk_out, dwv_out, hg_out, dg_out, sem):
    copies = []
    for src, dst in ((dwk, dwk_out), (dwv, dwv_out), (dq, dq_out)):
        step = src.shape[0] // 4
        for p in range(4):
            rows = pl.ds(p * step, step)
            cp = pltpu.make_async_copy(src.at[rows], dst.at[rows], sem.at[len(copies)])
            cp.start()
            copies.append(cp)
    hg_out[...] = hg[...]
    dg_out[...] = dg[...]
    for cp in copies:
        cp.wait()


def local(enc_hidden, enc_gain, key_weight, value_weight, queries, cotangent, enc_len, dec_len):
    vmem = pl.BlockSpec(memory_space=pltpu.VMEM)
    hbm = pl.BlockSpec(memory_space=pl.ANY)
    smem = pl.BlockSpec(memory_space=pltpu.SMEM)
    v = pltpu.VMEM
    shapes = (
        jax.ShapeDtypeStruct((DEC, WID), BF16),
        jax.ShapeDtypeStruct((QC, WID), BF16),
        jax.ShapeDtypeStruct((QC, WID), BF16),
        jax.ShapeDtypeStruct((8, D), BF16),
        jax.ShapeDtypeStruct((1, D), F32),
    )
    outs = pl.pallas_call(
        kernel,
        out_shape=tuple(v(o.shape, o.dtype) for o in shapes),
        in_specs=[vmem, vmem, hbm, hbm, vmem, vmem, smem, smem],
        out_specs=(vmem,) * 5,
        scratch_shapes=[
            v((D, WID), BF16),
            v((D, WID), BF16),
            pltpu.SemaphoreType.DMA((2,)),
            v((8, D), F32),
            v((8, D // 2), F32),
            v((4, NY, NZ, 16, QC), BF16),
            v((3, NY, NZ, 16, QC), BF16),
            v((ROWS, WID), F32),
            v((ROWS, WID), BF16),
            v((ROWS, WID), BF16),
            v((2, ROWS, DEC), F32),
            v((DEC, WID), BF16),
            v((2, ROWS, DEC), BF16),
            v((4, ROWS, WID), BF16),
            v((4, ROWS, WID), BF16),
            v((2, NY, NZ, 16, QC), BF16),
            v((2, NY, NZ, 16, QC), BF16),
            v((2, NY, NZ, 16, QC), F32),
            [v((3, NZ, 16, QC), BF16), v((3, 16, QC), BF16)],
            [v((7, 16, QC), BF16), v((8, 2, 2, 16, QC), BF16)],
            [v((3, NZ, 16, QC), BF16), v((3, 16, QC), BF16)],
            [v((7, 16, QC), BF16), v((8, 2, 2, 16, QC), BF16)],
            v((2, 2, 8, QC), F32),
            v((2, 8, QC), F32),
            v((QC, WID), F32),
            v((QC, WID), F32),
            v((NZ, 8, 256), F32),
            v((NY, 8, 256), F32),
            v((NX, 8, 256), F32),
            v((2, 8, 256), F32),
            pltpu.SemaphoreType.DMA((NSEND,)),
            pltpu.SemaphoreType.DMA((NSEM,)),
            pltpu.SemaphoreType.DMA((5,)),
            pltpu.SemaphoreType.DMA((6,)),
        ],
        compiler_params=pltpu.CompilerParams(
            collective_id=0, has_side_effects=True, vmem_limit_bytes=52 * 1024 * 1024
        ),
        cost_estimate=pl.CostEstimate(
            flops=15_000_000_000, bytes_accessed=12_000_000, transcendentals=300_000
        ),
    )(
        enc_hidden[0], enc_gain, key_weight[0, 0], value_weight[0, 0],
        queries[0, 0], cotangent[0, 0], enc_len, dec_len,
    )
    dq, dwk, dwv, hg, dg = pl.pallas_call(
        place,
        out_shape=shapes,
        in_specs=[vmem] * 5,
        out_specs=(hbm, hbm, hbm, vmem, vmem),
        scratch_shapes=[pltpu.SemaphoreType.DMA((12,))],
    )(*[pltpu.with_memory_space_constraint(o, pltpu.VMEM) for o in outs])
    return dq[None, None], dwk[None], dwv[None], hg[None], dg[0]


def solution(mesh):
    placed = (
        P("replica", ("section", "tensor"), None),
        P("replica", None),
        P("replica", "section", None, "tensor"),
        P("replica", "section", None, "tensor"),
        P("replica", "section", None, "tensor"),
        P("replica", "section", None, "tensor"),
        P("replica"),
        P("replica"),
    )
    return jax.shard_map(
        local,
        mesh=mesh,
        in_specs=placed,
        out_specs=(
            P("replica", "section", None, "tensor"),
            P("section", "replica", "tensor"),
            P("section", "replica", "tensor"),
            P("replica", ("section", "tensor"), None),
            P(),
        ),
        check_vma=False,
    )
```

time: 126 us -> 93.8 us (0.74)
  Pallas kernels: 116 us -> 91 us
  local copies, waits for them, and re-layouts: 7.47 us -> 0 us
    pallas_call x1 -> x2, Pallas kernels: 116 us -> 91 us  [the longest x1 88.9 us: local(): pl.pallas_call(kernel, out_shape=tuple((v(o.shape, o.dtype) for o in shap...]
    unnamed x9 -> x0, local copies, waits for them, and re-layouts: 7.47 us -> none
where the time goes in v2:
time: 93.8 us; the launch traced here: 93.1 us
  Pallas kernels  91 us (97%)
  between operations  2.09 us (2%)
    pallas_call x1, Pallas kernels, local(): pl.pallas_call(kernel, out_shape=tuple((v(o.shape, o.dtype) for o in shap...  88.9 us
    pallas_call x1, Pallas kernels, local(): pl.pallas_call(place, out_shape=shapes, in_specs=[vmem] * 5, out_specs=(h...  2.12 us

profile of v2, /device:TPU:1, one launch (start us, length us, event | category | flops | bytes accessed | tf_op | source)
XLA Modules:
  0.0 93.1 jit_solution(788334257140714153)
XLA Ops:
  1.9 88.9 %shard_map.119 = (bf16[256,512]{1,0:T(8,128)(2,1)S(1)}, bf16[1024,512]{1,0:T(8,128)(2,1)S(1)}, bf16[1024,512]{1,0:T(8,128)(2,1)S(1)}, bf16[8,4096]{1,0:T(8,128)(2,1)S(1)}, f32[1,4096]{1,0:T(1,128)S(1)}) custom-call(bf16[8,4096]{1,0:T(8,128)(2,1)} %bitcast.17, bf16[1,4096]{1,0:T(2,128)(2,1)} %gain_ref.1, bf16[4096,512]{1,0:T(8,128)(2,1)} %bitcast.10, ...), custom_call_target="tpu_custom_call" | custom-call | flops 15000000512 | bytes 12000000 | tf_op jit(solution)/shard_map/pallas_call | solution.py:509
  90.8 2.1 %shard_map.120 = (bf16[256,512]{1,0:T(8,128)(2,1)}, bf16[1024,512]{1,0:T(8,128)(2,1)}, bf16[1024,512]{1,0:T(8,128)(2,1)}, bf16[8,4096]{1,0:T(8,128)(2,1)}, f32[1,4096]{1,0:T(1,128)}) custom-call(bf16[256,512]{1,0:T(8,128)(2,1)S(1)} %get-tuple-element.15.dq, bf16[1024,512]{1,0:T(8,128)(2,1)S(1)} %get-tuple-element.16.dwk, ...), custom_call_target="tpu_custom_call" | custom-call | tf_op jit(solution)/shard_map/pallas_call | solution.py:560

commit v3 on v2

--- a/solution.py
+++ b/solution.py
@@ -15,8 +15,9 @@
 WID = 512
 NX, NY, NZ = 4, 4, 8
 QC = D // 4
+HC = QC // 2
 EC = QC // 4
-NSEM = 96
+NSEM = 173
 NSEND = 48
 
 
@@ -29,7 +30,7 @@
     dq_ref, dwk_ref, dwv_ref, hg_ref, dg_ref,
     wk, wv, wsem, n32, x32, G, E, acc, keys, vals, probs, grad, dsc, Dv, Dk,
     Ts, Tr, To, ly, lz, sy, sz, fin, dn, accv, acck,
-    gz, gy, gx, gf, ssem, rsem, esend, erecv,
+    gz, gy, gx, gf, ssem, rsem, esend, erecv, zsem,
 ):
     x = lax.axis_index("replica")
     sec = lax.axis_index("section")
@@ -101,7 +102,7 @@
     partners = [sibling]
     partners += [dev(dz=d) for d in range(1, NZ)]
     partners += [dev(dy=d) for d in range(1, NY)]
-    partners += [dev(dx=d) for d in range(1, NX)]
+    partners += [dev(dx=d, core=e) for d in range(1, NX) for e in (c, sib)]
     barrier = pltpu.get_barrier_semaphore()
     for p in partners:
         pl.semaphore_signal(barrier, inc=1, device_id=p, device_id_type=MESH)
@@ -124,95 +125,125 @@
     for j in range(2):
         G[2 * c + j, y, z] = chip[:, j * QC:(j + 1) * QC]
 
-    def ring8(half, landed):
-        a = [put(half(z, h), half(z, h), dev(dz=1)) for h in (0, 1)]
-        b = [put(half(z, h), half(z, h), dev(dz=-1)) for h in (1, 0)][::-1]
-        for k in (1, 2, 3):
-            yield
-            left, right = zo(-k), zo(k)
-            for far in (True, False):
-                ha, hb = (0, 1) if far else (1, 0)
-                got(a[ha], half(left, ha))
-                if k < 3 or far:
-                    a[ha] = put(half(left, ha), half(left, ha), dev(dz=1))
-                got(b[hb], half(right, hb))
-                if k < 3 or far:
-                    b[hb] = put(half(right, hb), half(right, hb), dev(dz=-1))
-            landed(left)
-            landed(right)
-        yield
-        got(a[0], half(zo(4), 0))
-        got(b[1], half(zo(4), 1))
-        landed(zo(4))
-
     arrivals = []
 
     def forward(region):
         i = put(region(c), region(c), sibling)
         arrivals.append((i, region(sib)))
 
-    def to_replica(j, at):
+    def cols_to(j, half):
         q = 2 * c + j
-
-        @pl.when(q != x)
-        def _():
-            slot = jnp.maximum(lax.rem(x - q + NX, NX) - 1, 0)
-            pltpu.make_async_remote_copy(
-                src_ref=G.at[(q,) + at], dst_ref=E.at[(slot,) + at],
-                send_sem=esend.at[j], recv_sem=erecv.at[slot],
-                device_id=dev(dx=q - x), device_id_type=MESH,
-            ).start()
-
+        slot = jnp.maximum(lax.rem(x - q + NX, NX) - 1, 0)
+        return pltpu.make_async_remote_copy(
+            src_ref=G.at[q, y, z, :, pl.ds(half * HC, HC)], dst_ref=E.at[half, slot, y, z],
+            send_sem=esend.at[2 * j + half], recv_sem=erecv.at[slot],
+            device_id=dev(dx=q - x, core=half), device_id_type=MESH,
+        )
+
+    def each_cols(act):
+        for j in range(2):
+            @pl.when(2 * c + j != x)
+            def _():
+                for half in range(2):
+                    act(cols_to(j, half))
+
+    ydist = (1, 3, 2)
+
+    def plane_gather(slab_a, slab_b, chunk_b, over_a, over_b):
+        def along_y(slab, zz):
+            return [put(slab(y, zz), slab(y, zz), dev(dy=d)) for d in ydist]
+
+        b_y = along_y(slab_b, z)
+        a_z = {d: put(slab_a(y, z), slab_a(y, z), dev(dz=d)) for d in (1, 7, 2, 6, 3, 5, 4)}
+        a_y = {0: along_y(slab_a, z)}
+
+        def from_z(*dist):
+            for d in dist:
+                got(a_z[d], slab_a(y, zo(-d)))
+                a_y[d] = along_y(slab_a, zo(-d))
+
+        def from_y(*dist):
+            for e in dist:
+                for d, i in zip(ydist, a_y[e]):
+                    got(i, slab_a(yo(-d), zo(-e)))
+
+        yield
+        from_z(1, 7)
+        for d, i in zip(ydist, b_y):
+            got(i, slab_b(yo(-d), z))
+        right = {h: put(chunk_b(z, h), chunk_b(z, h), dev(dz=1)) for h in (0, 1)}
+        left = {h: put(chunk_b(z, h), chunk_b(z, h), dev(dz=-1)) for h in (1, 0)}
+        forward(lambda cc: over_b(cc, z))
+
+        def hop(k):
+            for h in (0, 1):
+                zr, zl = zo(-k), zo(k)
+                if k < 4 or h == 0:
+                    got(right[h], chunk_b(zr, h))
+                    if k < 3 or (k == 3 and h == 0):
+                        right[h] = put(chunk_b(zr, h), chunk_b(zr, h), dev(dz=1))
+                g = 1 - h
+                if k < 4 or g == 1:
+                    got(left[g], chunk_b(zl, g))
+                    if k < 3 or (k == 3 and g == 1):
+                        left[g] = put(chunk_b(zl, g), chunk_b(zl, g), dev(dz=-1))
+            forward(lambda cc: over_b(cc, zo(-k)))
+            if k < 4:
+                forward(lambda cc: over_b(cc, zo(k)))
+
+        from_z(2, 6, 3, 5)
+        yield
+        hop(1)
+        from_z(4)
+        forward(lambda cc: over_a(cc, y))
+        yield
+        from_y(0, 1, 7)
+        hop(2)
+        yield
+        from_y(2, 6)
+        hop(3)
+        yield
+        from_y(3, 5, 4)
+        for d in ydist:
+            yy = yo(-d)
+            forward(lambda cc: over_a(cc, yy))
+        hop(4)
+
+    ga = plane_gather(
+        lambda yy, zz: G.at[2 * c, yy, zz],
+        lambda yy, zz: G.at[2 * c + 1, yy, zz],
+        lambda zz, h: G.at[2 * c + 1, pl.ds(2 * h, 2), zz],
+        lambda cc, yy: G.at[2 * cc, yy],
+        lambda cc, zz: G.at[2 * cc + 1, :, zz],
+    )
+    next(ga)
+    each_cols(lambda cp: cp.start())
+    for _ in ga:
+        pass
+    whole = list(arrivals)
+    arrivals.clear()
+
+    lo, hi = pl.ds(0, EC), pl.ds(EC, EC)
     every = slice(None)
-
-    def gather_z_first():
-        q = 2 * c
-        order = (4, 3, 5, 2, 6, 1, 7)
-        idx = [put(G.at[q, y, z], G.at[q, y, z], dev(dz=d)) for d in order]
-        yield
-        yield
-        for d, i in zip(order, idx):
-            got(i, G.at[q, y, zo(-d)])
-        order = (2, 1, 3)
-        idx = [put(G.at[q, y], G.at[q, y], dev(dy=d)) for d in order]
-        forward(lambda cc: G.at[2 * cc, y])
-        to_replica(0, (y,))
-        yield
-        yield
-        for d, i in zip(order, idx):
-            yy = yo(-d)
-            got(i, G.at[q, yy])
-            forward(lambda cc: G.at[2 * cc, yy])
-            to_replica(0, (yy,))
-
-    def gather_y_first():
-        q = 2 * c + 1
-        order = (2, 1, 3)
-        idx = [put(G.at[q, y, z], G.at[q, y, z], dev(dy=d)) for d in order]
-        yield
-        for d, i in zip(order, idx):
-            got(i, G.at[q, yo(-d), z])
-
-        def half(zz, h):
-            return G.at[q, pl.ds(2 * h, 2), zz]
-
-        def landed(zz):
-            forward(lambda cc: G.at[2 * cc + 1, :, zz])
-            to_replica(1, (every, zz))
-
-        first = ring8(half, landed)
-        next(first)
-        landed(z)
-        yield
-        yield from first
-
-    background += [gather_y_first(), gather_z_first()]
-    drain()
+    ea = plane_gather(
+        lambda yy, zz: E.at[c, :, yy, zz, :, lo],
+        lambda yy, zz: E.at[c, :, yy, zz, :, hi],
+        lambda zz, h: E.at[c, :, pl.ds(2 * h, 2), zz, :, hi],
+        lambda cc, yy: E.at[cc, :, yy, :, :, lo],
+        lambda cc, zz: E.at[cc, :, :, zz, :, hi],
+    )
+    for k in range(3):
+        slab = E.at[c, k, y, z]
+        pltpu.make_async_remote_copy(
+            src_ref=slab, dst_ref=slab, send_sem=esend.at[0], recv_sem=erecv.at[k],
+            device_id=sibling, device_id_type=MESH,
+        ).wait_recv()
+    next(ea)
 
     def project(w, out, first):
         for j in range(4):
             if first and j == 2:
-                for i, region in arrivals:
+                for i, region in whole:
                     got(i, region)
             q = lax.rem(2 * c + j, 4)
             part = dot(G[q].reshape(ROWS, QC), w[pl.ds(pl.multiple_of(q * QC, QC), QC), :])
@@ -269,6 +300,7 @@
     next(xv)
     wcopies[1].wait()
     project(wv, vals, False)
+    next(ea)
     for h in range(2):
         cols = slice(h * HD, (h + 1) * HD)
         dp = dot(vals[:, cols], grad[:, cols], 1, 1)
@@ -279,31 +311,46 @@
     xk = along_x(Dk)
     next(xk)
 
+    def slab_to(zz):
+        to = (x, (zz // 4 * NY + y) * 2 + c, zz % 4)
+        return pltpu.make_async_remote_copy(
+            src_ref=sz[0].at[zz], dst_ref=lz[0].at[z], send_sem=zsem.at[zz],
+            recv_sem=zsem.at[NZ], device_id=to, device_id_type=MESH,
+        )
+
     def sum_y_first():
         order = (2, 1, 3)
-        idx = []
-        for d in order:
-            sy[0][d - 1] = To[0, yo(d)].astype(BF16)
-            idx.append(put(sy[0].at[d - 1], ly[0].at[d - 1], dev(dy=d)))
-        yield
-        yield
-        for d, i in zip(order, idx):
-            got(i, ly[0].at[d - 1])
-        v = To[0, y]
-        for d in range(3):
-            v = v + ly[0][d].astype(F32)
-        To[0, y] = v
-        order = (4, 3, 5, 2, 6, 1, 7)
-        idx = []
-        for d in order:
-            sz[0][d - 1] = To[0, y, zo(d)].astype(BF16)
-            idx.append(put(sz[0].at[d - 1], lz[0].at[d - 1], dev(dz=d)))
-        yield
-        yield
-        for d, i in zip(order, idx):
-            got(i, lz[0].at[d - 1])
+        idx = {}
+        for h in range(2):
+            zs = pl.ds(4 * h, 4)
+            for d in order:
+                sy[0][d - 1, zs] = To[0, yo(d), zs].astype(BF16)
+                idx[h, d] = put(sy[0].at[d - 1, zs], ly[0].at[d - 1, zs], dev(dy=d))
+        lz[0][z] = jnp.zeros((16, QC), BF16)
+        yield
+        for h in range(2):
+            yield
+            zs = pl.ds(4 * h, 4)
+            for d in order:
+                got(idx[h, d], ly[0].at[d - 1, zs])
+            v = To[0, y, zs]
+            for d in range(3):
+                v = v + ly[0][d, zs].astype(F32)
+            To[0, y, zs] = v
+            sz[0][zs] = v.astype(BF16)
+            for zz in range(4 * h, 4 * h + 4):
+                @pl.when(zz != z)
+                def _():
+                    slab_to(zz).start()
+        yield
+        yield
+        got_all = lz[0].at[pl.ds(0, 7)]
+        pltpu.make_async_remote_copy(
+            src_ref=got_all, dst_ref=got_all, send_sem=zsem.at[0], recv_sem=zsem.at[NZ],
+            device_id=sibling, device_id_type=MESH,
+        ).wait_recv()
         v = To[0, y, z]
-        for d in range(7):
+        for d in range(NZ):
             v = v + lz[0][d].astype(F32)
         fin[0] = v.reshape(2, 8, QC)
 
@@ -350,19 +397,20 @@
             v = v + ly[1][d].astype(F32)
         fin[1] = v.reshape(2, 8, QC)
 
-    t_in = []
-    sums = [sum_y_first(), sum_z_first()]
-    for j in range(4):
-        q = lax.rem(2 * sib + j, 4)
-        w = pl.ds(pl.multiple_of(q * QC, QC), QC)
+    t_in = {}
+    sums = {1: sum_z_first(), 0: sum_y_first()}
+    for core, j in ((sib, 1), (sib, 0), (c, 1), (c, 0)):
+        w = pl.ds(pl.multiple_of((2 * core + j) * QC, QC), QC)
         t = dot(Dk[0], wk[w, :], 1, 1) + dot(Dv[0], wv[w, :], 1, 1)
-        if j < 2:
+        if core is sib:
             Ts[j] = t.astype(BF16).reshape(NY, NZ, 16, QC)
-            t_in.append(put(Ts.at[j], Tr.at[j], sibling))
+            t_in[j] = put(Ts.at[j], Tr.at[j], sibling)
         else:
-            got(t_in[j - 2], Tr.at[j - 2])
-            To[j - 2] = t.reshape(NY, NZ, 16, QC) + Tr[j - 2].astype(F32)
-            next(sums[j - 2])
+            got(t_in[j], Tr.at[j])
+            To[j] = t.reshape(NY, NZ, 16, QC) + Tr[j].astype(F32)
+            next(sums[j])
+        if j == 0:
+            next(ea)
     next(xv)
 
     gsel = jnp.where(c == 0, gain[:, :hc], gain[:, hc:])
@@ -397,10 +445,14 @@
                 dg_ref[0:1, lo:lo + 256] = gf[h, r:r + 1, :]
 
     def weight_part(buf, total, out, k):
-        src = G.at[x] if k == 0 else E.at[k - 1]
         for q in range(4):
             r = slice(q * EC, (q + 1) * EC)
-            part = dot(src[:, :, :, r].reshape(ROWS, EC), buf[k], 0, 0)
+            half = slice(q % 2 * EC, (q % 2 + 1) * EC)
+            if k == 0:
+                cols = G[x, :, :, :, r]
+            else:
+                cols = E[q // 2, k - 1, :, :, :, half]
+            part = dot(cols.reshape(ROWS, EC), buf[k], 0, 0)
             if k == 0:
                 total[r, :] = part
             elif k == 2:
@@ -408,40 +460,25 @@
             else:
                 total[r, :] += part
 
-    background += sums + [sum_gain()]
+    background += [sums[1], sums[0], sum_gain()]
     poll()
     for h in range(2):
         cols = slice(h * HD, (h + 1) * HD)
         dq_ref[:, cols] = (dot(dsc[h], keys[:, cols], 0, 0) * scale).astype(BF16)
     weight_part(Dv, accv, dwv_ref, 0)
     poll()
+    next(ea)
     weight_part(Dk, acck, dwk_ref, 0)
-
-    owner = lax.div(x, 2)
-    handed = []
-    for k in range(3):
-        def piece(send, recv):
-            return pltpu.make_async_remote_copy(
-                src_ref=E.at[k], dst_ref=E.at[k], send_sem=esend.at[send],
-                recv_sem=erecv.at[recv], device_id=sibling, device_id_type=MESH,
-            )
-
-        @pl.when(c == owner)
-        def _():
-            piece(2 + k, k).wait_recv()
-            piece(2 + k, 3 + k).start()
-
-        handed.append(piece(2 + k, 3 + k))
     poll()
+    next(ea, None)
     next(xv)
-    for cp in handed:
-        @pl.when(c != owner)
-        def _():
-            cp.wait_recv()
+    poll()
+    for i, region in arrivals:
+        got(i, region)
     weight_part(Dv, accv, dwv_ref, 1)
     weight_part(Dv, accv, dwv_ref, 3)
+    next(xk)
     poll()
-    next(xk)
     next(xv, None)
     weight_part(Dv, accv, dwv_ref, 2)
     drain()
@@ -465,17 +502,11 @@
     weight_part(Dk, acck, dwk_ref, 2)
     for cp in sends.values():
         cp.wait_send()
-    for j in range(2):
-        @pl.when(2 * c + j != x)
+    each_cols(lambda cp: cp.wait_send())
+    for d in range(NZ):
+        @pl.when(d != z)
         def _():
-            pltpu.make_async_remote_copy(
-                src_ref=G.at[2 * c + j], dst_ref=E.at[0], send_sem=esend.at[j],
-                recv_sem=erecv.at[0], device_id=sibling, device_id_type=MESH,
-            ).wait_send()
-    for cp in handed:
-        @pl.when(c == owner)
-        def _():
-            cp.wait_send()
+            slab_to(d).wait_send()
     assert count[0] == NSEM, count[0]
 
 
@@ -518,7 +549,7 @@
             v((8, D), F32),
             v((8, D // 2), F32),
             v((4, NY, NZ, 16, QC), BF16),
-            v((3, NY, NZ, 16, QC), BF16),
+            v((2, 3, NY, NZ, 16, HC), BF16),
             v((ROWS, WID), F32),
             v((ROWS, WID), BF16),
             v((ROWS, WID), BF16),
@@ -531,9 +562,9 @@
             v((2, NY, NZ, 16, QC), BF16),
             v((2, NY, NZ, 16, QC), F32),
             [v((3, NZ, 16, QC), BF16), v((3, 16, QC), BF16)],
-            [v((7, 16, QC), BF16), v((8, 2, 2, 16, QC), BF16)],
+            [v((NZ, 16, QC), BF16), v((8, 2, 2, 16, QC), BF16)],
             [v((3, NZ, 16, QC), BF16), v((3, 16, QC), BF16)],
-            [v((7, 16, QC), BF16), v((8, 2, 2, 16, QC), BF16)],
+            [v((NZ, 16, QC), BF16), v((8, 2, 2, 16, QC), BF16)],
             v((2, 2, 8, QC), F32),
             v((2, 8, QC), F32),
             v((QC, WID), F32),
@@ -544,8 +575,9 @@
             v((2, 8, 256), F32),
             pltpu.SemaphoreType.DMA((NSEND,)),
             pltpu.SemaphoreType.DMA((NSEM,)),
-            pltpu.SemaphoreType.DMA((5,)),
-            pltpu.SemaphoreType.DMA((6,)),
+            pltpu.SemaphoreType.DMA((4,)),
+            pltpu.SemaphoreType.DMA((3,)),
+            pltpu.SemaphoreType.DMA((NZ + 1,)),
         ],
         compiler_params=pltpu.CompilerParams(
             collective_id=0, has_side_effects=True, vmem_limit_bytes=52 * 1024 * 1024

time: 93.8 us -> 83.3 us (0.89)
  Pallas kernels: 91 us -> 81 us
    pallas_call x1, Pallas kernels: 88.9 us -> 78.9 us  [local(): pl.pallas_call(kernel, out_shape=tuple((v(o.shape, o.dtype) for o in shap...]
where the time goes in v3:
time: 83.3 us; the launch traced here: 83.1 us
  Pallas kernels  81 us (97%)
  between operations  2.09 us (3%)
    pallas_call x1, Pallas kernels, local(): pl.pallas_call(kernel, out_shape=tuple((v(o.shape, o.dtype) for o in shap...  78.9 us
    pallas_call x1, Pallas kernels, local(): pl.pallas_call(place, out_shape=shapes, in_specs=[vmem] * 5, out_specs=(h...  2.12 us

profile of v3, /device:TPU:1, one launch (start us, length us, event | category | flops | bytes accessed | tf_op | source)
XLA Modules:
  0.0 83.1 jit_solution(13776317031610843190)
XLA Ops:
  1.9 78.9 %shard_map.119 = (bf16[256,512]{1,0:T(8,128)(2,1)S(1)}, bf16[1024,512]{1,0:T(8,128)(2,1)S(1)}, bf16[1024,512]{1,0:T(8,128)(2,1)S(1)}, bf16[8,4096]{1,0:T(8,128)(2,1)S(1)}, f32[1,4096]{1,0:T(1,128)S(1)}) custom-call(bf16[8,4096]{1,0:T(8,128)(2,1)} %bitcast.17, bf16[1,4096]{1,0:T(2,128)(2,1)} %gain_ref.1, bf16[4096,512]{1,0:T(8,128)(2,1)} %bitcast.10, ...), custom_call_target="tpu_custom_call" | custom-call | flops 15000000512 | bytes 12000000 | tf_op jit(solution)/shard_map/pallas_call | solution.py:540
  80.8 2.1 %shard_map.120 = (bf16[256,512]{1,0:T(8,128)(2,1)}, bf16[1024,512]{1,0:T(8,128)(2,1)}, bf16[1024,512]{1,0:T(8,128)(2,1)}, bf16[8,4096]{1,0:T(8,128)(2,1)}, f32[1,4096]{1,0:T(1,128)}) custom-call(bf16[256,512]{1,0:T(8,128)(2,1)S(1)} %get-tuple-element.15.dq, bf16[1024,512]{1,0:T(8,128)(2,1)S(1)} %get-tuple-element.16.dwk, ...), custom_call_target="tpu_custom_call" | custom-call | tf_op jit(solution)/shard_map/pallas_call | solution.py:592

commit v4 on v3

--- a/solution.py
+++ b/solution.py
@@ -17,8 +17,8 @@
 QC = D // 4
 HC = QC // 2
 EC = QC // 4
-NSEM = 173
-NSEND = 48
+NSEM = 89
+NSEND = 112
 
 
 def dot(a, b, ca=1, cb=0):
@@ -26,9 +26,9 @@
 
 
 def kernel(
-    hid_ref, gain_ref, kw_ref, vw_ref, q_ref, ct_ref, elen_ref, dlen_ref,
+    hid_ref, gain_ref, kw_ref, vw_ref, q_ref, ct_ref, elen_hbm, dlen_hbm,
     dq_ref, dwk_ref, dwv_ref, hg_ref, dg_ref,
-    wk, wv, wsem, n32, x32, G, E, acc, keys, vals, probs, grad, dsc, Dv, Dk,
+    wk, wv, wsem, elen_ref, dlen_ref, n32, x32, G, E, acc, keys, vals, probs, grad, dsc, Dv, Dk,
     Ts, Tr, To, ly, lz, sy, sz, fin, dn, accv, acck,
     gz, gy, gx, gf, ssem, rsem, esend, erecv, zsem,
 ):
@@ -58,12 +58,17 @@
 
     sibling = dev(core=sib)
     count = [0]
+    order = [0]
     sends = {}
 
-    def put(src, dst, to):
-        i = count[0]
+    def group():
         count[0] += 1
-        s = i % NSEND
+        return count[0] - 1
+
+    def put(src, dst, to, i=None):
+        i = group() if i is None else i
+        s = order[0] % NSEND
+        order[0] += 1
         if s in sends:
             sends[s].wait_send()
         cp = pltpu.make_async_remote_copy(
@@ -95,6 +100,8 @@
     wcopies = [
         pltpu.make_async_copy(kw_ref, wk, wsem.at[0]),
         pltpu.make_async_copy(vw_ref, wv, wsem.at[1]),
+        pltpu.make_async_copy(elen_hbm, elen_ref, wsem.at[2]),
+        pltpu.make_async_copy(dlen_hbm, dlen_ref, wsem.at[3]),
     ]
     for w in wcopies:
         w.start()
@@ -125,12 +132,6 @@
     for j in range(2):
         G[2 * c + j, y, z] = chip[:, j * QC:(j + 1) * QC]
 
-    arrivals = []
-
-    def forward(region):
-        i = put(region(c), region(c), sibling)
-        arrivals.append((i, region(sib)))
-
     def cols_to(j, half):
         q = 2 * c + j
         slot = jnp.maximum(lax.rem(x - q + NX, NX) - 1, 0)
@@ -149,28 +150,33 @@
 
     ydist = (1, 3, 2)
 
-    def plane_gather(slab_a, slab_b, chunk_b, over_a, over_b):
-        def along_y(slab, zz):
-            return [put(slab(y, zz), slab(y, zz), dev(dy=d)) for d in ydist]
-
-        b_y = along_y(slab_b, z)
+    def plane_gather(slab_a, half_a, slab_b, chunk_b, over_a, over_b, some_a, some_b, over):
+        def forward(region):
+            put(region(c), region(c), sibling, over)
+
+        def along_y(slab, zz, i):
+            for d in ydist:
+                put(slab(y, zz), slab(y, zz), dev(dy=d), i)
+
+        b_y = group()
+        along_y(slab_b, z, b_y)
         a_z = {d: put(slab_a(y, z), slab_a(y, z), dev(dz=d)) for d in (1, 7, 2, 6, 3, 5, 4)}
-        a_y = {0: along_y(slab_a, z)}
+        a_y = {e: group() for e in (0, 2, 3)}
+        group_of = {0: 0, 1: 0, 7: 0, 2: 2, 6: 2, 3: 3, 5: 3, 4: 3}
+        along_y(slab_a, z, a_y[0])
 
         def from_z(*dist):
             for d in dist:
-                got(a_z[d], slab_a(y, zo(-d)))
-                a_y[d] = along_y(slab_a, zo(-d))
-
-        def from_y(*dist):
-            for e in dist:
-                for d, i in zip(ydist, a_y[e]):
-                    got(i, slab_a(yo(-d), zo(-e)))
+                zz = zo(-d)
+                got(a_z[d], slab_a(y, zz))
+                along_y(slab_a, zz, a_y[group_of[d]])
+
+        def from_y(e, n):
+            got(a_y[e], some_a(n))
 
         yield
         from_z(1, 7)
-        for d, i in zip(ydist, b_y):
-            got(i, slab_b(yo(-d), z))
+        got(b_y, some_b())
         right = {h: put(chunk_b(z, h), chunk_b(z, h), dev(dz=1)) for h in (0, 1)}
         left = {h: put(chunk_b(z, h), chunk_b(z, h), dev(dz=-1)) for h in (1, 0)}
         forward(lambda cc: over_b(cc, z))
@@ -197,40 +203,47 @@
         from_z(4)
         forward(lambda cc: over_a(cc, y))
         yield
-        from_y(0, 1, 7)
+        from_y(0, 3)
         hop(2)
         yield
-        from_y(2, 6)
+        from_y(2, 2)
         hop(3)
         yield
-        from_y(3, 5, 4)
+        from_y(3, 3)
         for d in ydist:
             yy = yo(-d)
             forward(lambda cc: over_a(cc, yy))
         hop(4)
 
+    g_over, e_over = group(), group()
     ga = plane_gather(
         lambda yy, zz: G.at[2 * c, yy, zz],
+        lambda yy, zz, h: G.at[2 * c, yy, zz, :, pl.ds(h * HC, HC)],
         lambda yy, zz: G.at[2 * c + 1, yy, zz],
         lambda zz, h: G.at[2 * c + 1, pl.ds(2 * h, 2), zz],
         lambda cc, yy: G.at[2 * cc, yy],
         lambda cc, zz: G.at[2 * cc + 1, :, zz],
+        lambda n: G.at[2 * c, pl.ds(0, 3), pl.ds(0, n)],
+        lambda: G.at[2 * c + 1, pl.ds(0, 3), z],
+        g_over,
     )
     next(ga)
     each_cols(lambda cp: cp.start())
     for _ in ga:
         pass
-    whole = list(arrivals)
-    arrivals.clear()
 
     lo, hi = pl.ds(0, EC), pl.ds(EC, EC)
     every = slice(None)
     ea = plane_gather(
         lambda yy, zz: E.at[c, :, yy, zz, :, lo],
+        lambda yy, zz, h: E.at[c, :, yy, zz, :, pl.ds(h * (EC // 2), EC // 2)],
         lambda yy, zz: E.at[c, :, yy, zz, :, hi],
         lambda zz, h: E.at[c, :, pl.ds(2 * h, 2), zz, :, hi],
         lambda cc, yy: E.at[cc, :, yy, :, :, lo],
         lambda cc, zz: E.at[cc, :, :, zz, :, hi],
+        lambda n: E.at[c, :, pl.ds(0, 3), pl.ds(0, n), :, lo],
+        lambda: E.at[c, :, pl.ds(0, 3), z, :, hi],
+        e_over,
     )
     for k in range(3):
         slab = E.at[c, k, y, z]
@@ -243,8 +256,7 @@
     def project(w, out, first):
         for j in range(4):
             if first and j == 2:
-                for i, region in whole:
-                    got(i, region)
+                got(g_over, G.at[pl.ds(2 * sib, 2)])
             q = lax.rem(2 * c + j, 4)
             part = dot(G[q].reshape(ROWS, QC), w[pl.ds(pl.multiple_of(q * QC, QC), QC), :])
             if j == 0:
@@ -261,6 +273,8 @@
     row_z = (row >> 4) & 7
     row_y = row >> 7
     pos = ((((row_z >> 2) * NY + row_y) * 2 + row_c) * 4 + (row_z & 3)) * 8 + inner
+    wcopies[2].wait()
+    wcopies[3].wait()
     keep = pos < elen_ref[0]
     live = lax.broadcasted_iota(jnp.int32, (DEC, 1), 0) < dlen_ref[0]
     grad[...] = jnp.where(live, ct_ref[...], jnp.zeros((DEC, WID), BF16))
@@ -320,19 +334,18 @@
 
     def sum_y_first():
         order = (2, 1, 3)
-        idx = {}
+        idx = [group(), group()]
         for h in range(2):
             zs = pl.ds(4 * h, 4)
             for d in order:
                 sy[0][d - 1, zs] = To[0, yo(d), zs].astype(BF16)
-                idx[h, d] = put(sy[0].at[d - 1, zs], ly[0].at[d - 1, zs], dev(dy=d))
+                put(sy[0].at[d - 1, zs], ly[0].at[d - 1, zs], dev(dy=d), idx[h])
         lz[0][z] = jnp.zeros((16, QC), BF16)
         yield
         for h in range(2):
             yield
             zs = pl.ds(4 * h, 4)
-            for d in order:
-                got(idx[h, d], ly[0].at[d - 1, zs])
+            got(idx[h], ly[0].at[:, zs])
             v = To[0, y, zs]
             for d in range(3):
                 v = v + ly[0][d, zs].astype(F32)
@@ -385,13 +398,12 @@
                 own(z, h) + land[3, h].astype(F32) + land[7, h].astype(F32)
             )
         order = (2, 1, 3)
-        idx = []
+        i = group()
         for d in order:
             sy[1][d - 1] = To[1, yo(d), z].astype(BF16)
-            idx.append(put(sy[1].at[d - 1], ly[1].at[d - 1], dev(dy=d)))
-        yield
-        for d, i in zip(order, idx):
-            got(i, ly[1].at[d - 1])
+            put(sy[1].at[d - 1], ly[1].at[d - 1], dev(dy=d), i)
+        yield
+        got(i, ly[1])
         v = To[1, y, z]
         for d in range(3):
             v = v + ly[1][d].astype(F32)
@@ -421,20 +433,23 @@
             gz[z, 4 * j + r:4 * j + r + 1, :] = terms[:, r * 256:(r + 1) * 256]
 
     def sum_gain():
-        idx = [(put(gz.at[z], gz.at[z], dev(dz=d)), zo(-d)) for d in range(1, NZ)]
-        yield
-        for i, s in idx:
-            got(i, gz.at[s])
+        def spread(buf, me, to, n):
+            i = group()
+            for d in range(1, n):
+                put(buf.at[me], buf.at[me], to(d), i)
+            return i
+
+        i = spread(gz, z, lambda d: dev(dz=d), NZ)
+        yield
+        got(i, gz.at[pl.ds(0, NZ - 1)])
         gy[y] = jnp.sum(gz[...], axis=0)
-        idx = [(put(gy.at[y], gy.at[y], dev(dy=d)), yo(-d)) for d in range(1, NY)]
-        yield
-        for i, s in idx:
-            got(i, gy.at[s])
+        i = spread(gy, y, lambda d: dev(dy=d), NY)
+        yield
+        got(i, gy.at[pl.ds(0, NY - 1)])
         gx[x] = jnp.sum(gy[...], axis=0)
-        idx = [(put(gx.at[x], gx.at[x], dev(dx=d)), xo(-d)) for d in range(1, NX)]
-        yield
-        for i, s in idx:
-            got(i, gx.at[s])
+        i = spread(gx, x, lambda d: dev(dx=d), NX)
+        yield
+        got(i, gx.at[pl.ds(0, NX - 1)])
         gf[c] = jnp.sum(gx[...], axis=0) / NX
         i = put(gf.at[c], gf.at[c], sibling)
         yield
@@ -460,30 +475,38 @@
             else:
                 total[r, :] += part
 
-    background += [sums[1], sums[0], sum_gain()]
+    background += [sums[1], sums[0]]
+    gain_sum = sum_gain()
     poll()
+    next(gain_sum)
     for h in range(2):
         cols = slice(h * HD, (h + 1) * HD)
         dq_ref[:, cols] = (dot(dsc[h], keys[:, cols], 0, 0) * scale).astype(BF16)
     weight_part(Dv, accv, dwv_ref, 0)
     poll()
+    next(gain_sum)
     next(ea)
     weight_part(Dk, acck, dwk_ref, 0)
     poll()
+    next(gain_sum)
     next(ea, None)
     next(xv)
     poll()
-    for i, region in arrivals:
-        got(i, region)
+    got(e_over, E.at[sib])
     weight_part(Dv, accv, dwv_ref, 1)
     weight_part(Dv, accv, dwv_ref, 3)
     next(xk)
     poll()
     next(xv, None)
     weight_part(Dv, accv, dwv_ref, 2)
+    poll()
+    next(gain_sum)
     drain()
 
     i = put(fin.at[:, sib], dn, sibling)
+    next(xk)
+    weight_part(Dk, acck, dwk_ref, 1)
+    weight_part(Dk, acck, dwk_ref, 3)
     got(i, dn)
     own_half = jnp.concatenate([fin[0, c], fin[1, c]], axis=1)
     other_half = jnp.concatenate([dn[0], dn[1]], axis=1)
@@ -494,10 +517,7 @@
     scaled = gain * dnorm
     hg = (scaled - xhat * jnp.mean(scaled * xhat, axis=-1, keepdims=True)) / rms
     hg_ref[...] = hg.astype(BF16)
-
-    next(xk)
-    weight_part(Dk, acck, dwk_ref, 1)
-    weight_part(Dk, acck, dwk_ref, 3)
+    next(gain_sum, None)
     next(xk, None)
     weight_part(Dk, acck, dwk_ref, 2)
     for cp in sends.values():
@@ -528,7 +548,6 @@
 def local(enc_hidden, enc_gain, key_weight, value_weight, queries, cotangent, enc_len, dec_len):
     vmem = pl.BlockSpec(memory_space=pltpu.VMEM)
     hbm = pl.BlockSpec(memory_space=pl.ANY)
-    smem = pl.BlockSpec(memory_space=pltpu.SMEM)
     v = pltpu.VMEM
     shapes = (
         jax.ShapeDtypeStruct((DEC, WID), BF16),
@@ -540,12 +559,14 @@
     outs = pl.pallas_call(
         kernel,
         out_shape=tuple(v(o.shape, o.dtype) for o in shapes),
-        in_specs=[vmem, vmem, hbm, hbm, vmem, vmem, smem, smem],
+        in_specs=[vmem, vmem, hbm, hbm, vmem, vmem, hbm, hbm],
         out_specs=(vmem,) * 5,
         scratch_shapes=[
             v((D, WID), BF16),
             v((D, WID), BF16),
-            pltpu.SemaphoreType.DMA((2,)),
+            pltpu.SemaphoreType.DMA((4,)),
+            pltpu.SMEM((1,), jnp.int32),
+            pltpu.SMEM((1,), jnp.int32),
             v((8, D), F32),
             v((8, D // 2), F32),
             v((4, NY, NZ, 16, QC), BF16),

time: 83.3 us -> 82.1 us (0.986)
  Pallas kernels: 81 us -> 79.9 us
    pallas_call x1, Pallas kernels: 78.9 us -> 77.8 us  [local(): pl.pallas_call(kernel, out_shape=tuple((v(o.shape, o.dtype) for o in shap...]
where the time goes in v4:
time: 82.1 us; the launch traced here: 82 us
  Pallas kernels  79.9 us (97%)
  between operations  2.09 us (3%)
    pallas_call x1, Pallas kernels, local(): pl.pallas_call(kernel, out_shape=tuple((v(o.shape, o.dtype) for o in shap...  77.8 us
    pallas_call x1, Pallas kernels, local(): pl.pallas_call(place, out_shape=shapes, in_specs=[vmem] * 5, out_specs=(h...  2.12 us

profile of v4, /device:TPU:1, one launch (start us, length us, event | category | flops | bytes accessed | tf_op | source)
XLA Modules:
  0.0 82.0 jit_solution(5220489601443738090)
XLA Ops:
  1.9 77.8 %shard_map.119 = (bf16[256,512]{1,0:T(8,128)(2,1)S(1)}, bf16[1024,512]{1,0:T(8,128)(2,1)S(1)}, bf16[1024,512]{1,0:T(8,128)(2,1)S(1)}, bf16[8,4096]{1,0:T(8,128)(2,1)S(1)}, f32[1,4096]{1,0:T(1,128)S(1)}) custom-call(bf16[8,4096]{1,0:T(8,128)(2,1)} %bitcast.17, bf16[1,4096]{1,0:T(2,128)(2,1)} %gain_ref.1, bf16[4096,512]{1,0:T(8,128)(2,1)} %bitcast.10, ...), custom_call_target="tpu_custom_call" | custom-call | flops 15000000512 | bytes 12000000 | tf_op jit(solution)/shard_map/pallas_call | solution.py:559
  79.7 2.1 %shard_map.120 = (bf16[256,512]{1,0:T(8,128)(2,1)}, bf16[1024,512]{1,0:T(8,128)(2,1)}, bf16[1024,512]{1,0:T(8,128)(2,1)}, bf16[8,4096]{1,0:T(8,128)(2,1)}, f32[1,4096]{1,0:T(1,128)}) custom-call(bf16[256,512]{1,0:T(8,128)(2,1)S(1)} %get-tuple-element.15.dq, bf16[1024,512]{1,0:T(8,128)(2,1)S(1)} %get-tuple-element.16.dwk, ...), custom_call_target="tpu_custom_call" | custom-call | tf_op jit(solution)/shard_map/pallas_call | solution.py:613

commit v5 on v4

--- a/solution.py
+++ b/solution.py
@@ -213,6 +213,7 @@
         for d in ydist:
             yy = yo(-d)
             forward(lambda cc: over_a(cc, yy))
+        yield
         hop(4)
 
     g_over, e_over = group(), group()
@@ -229,6 +230,12 @@
     )
     next(ga)
     each_cols(lambda cp: cp.start())
+    for _ in range(5):
+        next(ga)
+    wcopies[0].wait()
+    acc[...] = dot(
+        G[2 * c].reshape(ROWS, QC), wk[pl.ds(pl.multiple_of(2 * c * QC, QC), QC), :]
+    )
     for _ in ga:
         pass
 
@@ -254,7 +261,7 @@
     next(ea)
 
     def project(w, out, first):
-        for j in range(4):
+        for j in range(1 if first else 0, 4):
             if first and j == 2:
                 got(g_over, G.at[pl.ds(2 * sib, 2)])
             q = lax.rem(2 * c + j, 4)
@@ -278,7 +285,6 @@
     keep = pos < elen_ref[0]
     live = lax.broadcasted_iota(jnp.int32, (DEC, 1), 0) < dlen_ref[0]
     grad[...] = jnp.where(live, ct_ref[...], jnp.zeros((DEC, WID), BF16))
-    wcopies[0].wait()
     project(wk, keys, True)
     for h in range(2):
         cols = slice(h * HD, (h + 1) * HD)
@@ -489,7 +495,8 @@
     weight_part(Dk, acck, dwk_ref, 0)
     poll()
     next(gain_sum)
-    next(ea, None)
+    for _ in ea:
+        pass
     next(xv)
     poll()
     got(e_over, E.at[sib])

time: 82.1 us -> 82.3 us (level)
  no operation moved by 1% of the time
where the time goes in v5:
time: 82.3 us; the launch traced here: 82.1 us
  Pallas kernels  80.1 us (97%)
  between operations  2.09 us (3%)
    pallas_call x1, Pallas kernels, local(): pl.pallas_call(kernel, out_shape=tuple((v(o.shape, o.dtype) for o in shap...  77.9 us
    pallas_call x1, Pallas kernels, local(): pl.pallas_call(place, out_shape=shapes, in_specs=[vmem] * 5, out_specs=(h...  2.12 us

profile of v5, /device:TPU:1, one launch (start us, length us, event | category | flops | bytes accessed | tf_op | source)
XLA Modules:
  0.0 82.1 jit_solution(2175656214552786727)
XLA Ops:
  1.9 77.9 %shard_map.119 = (bf16[256,512]{1,0:T(8,128)(2,1)S(1)}, bf16[1024,512]{1,0:T(8,128)(2,1)S(1)}, bf16[1024,512]{1,0:T(8,128)(2,1)S(1)}, bf16[8,4096]{1,0:T(8,128)(2,1)S(1)}, f32[1,4096]{1,0:T(1,128)S(1)}) custom-call(bf16[8,4096]{1,0:T(8,128)(2,1)} %bitcast.17, bf16[1,4096]{1,0:T(2,128)(2,1)} %gain_ref.1, bf16[4096,512]{1,0:T(8,128)(2,1)} %bitcast.10, ...), custom_call_target="tpu_custom_call" | custom-call | flops 15000000512 | bytes 12000000 | tf_op jit(solution)/shard_map/pallas_call | solution.py:566
  79.9 2.1 %shard_map.120 = (bf16[256,512]{1,0:T(8,128)(2,1)}, bf16[1024,512]{1,0:T(8,128)(2,1)}, bf16[1024,512]{1,0:T(8,128)(2,1)}, bf16[8,4096]{1,0:T(8,128)(2,1)}, f32[1,4096]{1,0:T(1,128)}) custom-call(bf16[256,512]{1,0:T(8,128)(2,1)S(1)} %get-tuple-element.15.dq, bf16[1024,512]{1,0:T(8,128)(2,1)S(1)} %get-tuple-element.16.dwk, ...), custom_call_target="tpu_custom_call" | custom-call | tf_op jit(solution)/shard_map/pallas_call | solution.py:620
